TPU v7x, 128 devices: a whole 4x4x4 slice. The times are simulated.
128 devices in a mesh: expo: 4 (over y), fp: 32 (over x, z, core).
Axes of the slice: x: 4, y: 4, z: 4, core: 2. Of those that a mesh axis runs over, the one named last changes fastest.
Arguments:
- raw_pixels: bfloat16 [4, 8192, 2048], P('expo', 'fp'), may hold values from -6 to 6
- kernel_bank: bfloat16 [8, 2, 41], replicated, may hold values from -1 to 1
- kernel_ids: int32 [4, 32], P('expo', 'fp'), may hold values from 0 to 7
- inv_var: float32 [4, 32], P('expo', 'fp'), may hold values from 0.3 to 3
- gap_start: int32 [4, 32], P('expo', 'fp'), may hold values from 0 to 224
- warp_tile: int32 [4, 8192, 16, 1], P('expo', 'fp'), may hold values from 0 to 127; in each aligned block of 4096 rows (0 to 4095, 4096 to 8191, ..., all dimensions but the last counted through in order) at most 64 rows name the same one
- warp_offset: int32 [4, 8192, 16], P('expo', 'fp'), may hold values from 0 to 4095
Outputs:
- coadd_image: float32 [128, 4096, 128], P(('expo', 'fp'))
- coadd_weight: float32 [128, 4096], P(('expo', 'fp'))
Inputs may be any that keep to these rules, and one draw needn't show every extreme that they name: `warp_tile`: among the 4096 row segments of one exposure's CCD window (256 pixel rows of 16 segments each), at most 64 go to one tile, and in some windows exactly 64 do.
All inputs are finite; a program needn't handle non-finite values.
Results may differ from a plain program's by a relative error of at most 0.006.
Values may be sent and summed in bfloat16 or wider, within the bound.
A program may use at most 64 MiB of HBM per device.

v0:
```python
import math

import jax
import jax.numpy as jnp
from jax import lax
from jax.sharding import PartitionSpec as P

GAP = 32


def padded_2(shard, sides, width):
    for axis, dim in sides:
        size, length = (lax.axis_size(axis), shard.shape[dim])
        up = [(i, (i + 1) % size) for i in range(size - 1)]
        down = [(j, i) for i, j in up]
        last = lax.slice_in_dim(shard, length - width, length, axis=dim)
        first = lax.slice_in_dim(shard, 0, width, axis=dim)
        before = lax.ppermute(last, axis, up)
        after = lax.ppermute(first, axis, down)
        shard = jnp.concatenate([before, shard, after], axis=dim)
    return shard


def toeplitz(tap_table, offset):
    tap_total = tap_table.shape[1]
    row_pos = jnp.arange(128)[:, None]
    col_pos = jnp.arange(128)[None, :]
    where_tap = offset + row_pos - col_pos
    band = (where_tap[None, :, :] == jnp.arange(tap_total)[:, None, None]).astype(jnp.bfloat16)
    built = jnp.einsum("et,tab->eab", tap_table, band, preferred_element_type=jnp.float32)
    return built.astype(jnp.bfloat16)


def body(raw_pixels, kernel_bank, kernel_ids, inv_var, gap_start, warp_tile, warp_offset):
    e_dev, row_count, col_count = raw_pixels.shape
    block_width = 128
    half_taps = kernel_bank.shape[2] // 2
    row_blocks = row_count // block_width
    col_blocks = col_count // block_width
    selector = (kernel_ids == jnp.arange(kernel_bank.shape[0])[None, :]).astype(jnp.float32)
    tap_table = jnp.einsum("ek,kst->est", selector, kernel_bank.astype(jnp.float32)).astype(
        jnp.bfloat16
    )
    padded = padded_2(raw_pixels, (("fp", 1),), half_taps)
    padded = jnp.pad(padded, ((0, 0), (0, block_width - 2 * half_taps), (0, 0)))
    stacked = padded.reshape(e_dev, row_blocks + 1, block_width, col_count)
    upper_matrix = toeplitz(tap_table[:, 0], 0)
    lower_matrix = toeplitz(tap_table[:, 0], block_width)
    vertical = jnp.einsum(
        "eiac,eab->eibc", stacked[:, :row_blocks], upper_matrix, preferred_element_type=jnp.float32
    )
    vertical = vertical + jnp.einsum(
        "eiac,eab->eibc", stacked[:, 1:], lower_matrix, preferred_element_type=jnp.float32
    )
    vertical = vertical.reshape(e_dev, row_count, col_blocks, block_width).astype(jnp.bfloat16)
    framed = jnp.pad(vertical, ((0, 0), (0, 0), (1, 1), (0, 0)))
    filtered = jnp.zeros((e_dev, row_count, col_blocks, block_width), jnp.float32)
    for block_shift in (-1, 0, 1):
        matrix = toeplitz(tap_table[:, 1], block_width * block_shift + half_taps)
        filtered = filtered + jnp.einsum(
            "erja,eab->erjb",
            framed[:, :, 1 + block_shift : 1 + block_shift + col_blocks],
            matrix,
            preferred_element_type=jnp.float32,
        )
    convolved = filtered.astype(jnp.bfloat16).reshape(e_dev, row_count * col_blocks, block_width)
    row_index = jnp.arange(row_count)[None, :]
    in_gap = (row_index >= gap_start) & (row_index < gap_start + GAP)
    row_weight = jnp.where(in_gap, jnp.zeros((), jnp.float32), inv_var)
    piece_weight = jnp.broadcast_to(row_weight[:, :, None], (e_dev, row_count, col_blocks)).reshape(
        e_dev, -1
    )
    targets = warp_tile.reshape(e_dev, -1)
    offsets = warp_offset.reshape(e_dev, -1)
    pieces = targets.shape[1]
    devices = lax.axis_size("expo") * lax.axis_size("fp")
    capacity = max(2, 2 * pieces // devices)
    owner_hot = (targets[:, :, None] == jnp.arange(devices)[None, None, :]).astype(jnp.bfloat16)
    piece_groups = pieces // 128
    grouped_hot = owner_hot.reshape(e_dev, piece_groups, 128, devices)
    strictly_lower = (jnp.arange(128)[:, None] > jnp.arange(128)[None, :]).astype(jnp.bfloat16)
    inside_rank = jnp.einsum(
        "ab,enbd->enad", strictly_lower, grouped_hot, preferred_element_type=jnp.float32
    )
    group_totals = jnp.sum(grouped_hot.astype(jnp.float32), axis=2)
    group_before = jnp.cumsum(group_totals, axis=1) - group_totals
    rank_value = jnp.sum(
        grouped_hot.astype(jnp.float32) * (inside_rank + group_before[:, :, None, :]), axis=3
    )
    destination = targets * capacity + rank_value.reshape(e_dev, pieces).astype(jnp.int32)
    send_slots = devices * capacity
    send_block = math.gcd(send_slots, 1024)

    def pack_block(block_number):
        slot_index = block_number * send_block + jnp.arange(send_block)
        matched = destination[:, None, :] == slot_index[None, :, None]
        values = jnp.einsum(
            "ebp,epc->ebc",
            matched.astype(jnp.bfloat16),
            convolved,
            preferred_element_type=jnp.float32,
        ).astype(jnp.bfloat16)
        slot_offsets = jnp.sum(jnp.where(matched, offsets[:, None, :], 0), axis=2)
        slot_weights = jnp.sum(
            jnp.where(matched, piece_weight[:, None, :], jnp.zeros((), jnp.float32)), axis=2
        )
        return (values, slot_offsets, slot_weights)

    packed_values, packed_offsets, packed_weights = lax.map(
        pack_block, jnp.arange(send_slots // send_block)
    )
    send_values = jnp.transpose(
        jnp.transpose(packed_values, (1, 0, 2, 3)).reshape(e_dev, devices, capacity, block_width),
        (1, 0, 2, 3),
    )
    send_offsets = jnp.transpose(
        jnp.transpose(packed_offsets, (1, 0, 2)).reshape(e_dev, devices, capacity), (1, 0, 2)
    )
    send_weights = jnp.transpose(
        jnp.transpose(packed_weights, (1, 0, 2)).reshape(e_dev, devices, capacity), (1, 0, 2)
    )
    got_values, got_offsets, got_weights = (
        lax.all_to_all(send_values, ("expo", "fp"), split_axis=0, concat_axis=0, tiled=True),
        lax.all_to_all(send_offsets, ("expo", "fp"), split_axis=0, concat_axis=0, tiled=True),
        lax.all_to_all(
            send_weights.astype(jnp.bfloat16),
            ("expo", "fp"),
            split_axis=0,
            concat_axis=0,
            tiled=True,
        ).astype(send_weights.dtype),
    )
    flat_values = got_values.reshape(-1, block_width)
    flat_offsets = got_offsets.reshape(-1)
    flat_weights = got_weights.reshape(-1)
    products = flat_weights[:, None] * flat_values.astype(jnp.float32)
    upper_part = products.astype(jnp.bfloat16)
    lower_part = (products - upper_part.astype(jnp.float32)).astype(jnp.bfloat16)
    both_parts = jnp.concatenate([upper_part, lower_part], axis=1)
    sum_block_rows = math.gcd(pieces, 512)

    def sum_block(block_number):
        slot_index = block_number * sum_block_rows + jnp.arange(sum_block_rows)
        matched = slot_index[:, None] == flat_offsets[None, :]
        summed = jnp.dot(
            matched.astype(jnp.bfloat16), both_parts, preferred_element_type=jnp.float32
        )
        image_rows = summed[:, :block_width] + summed[:, block_width:]
        weight_rows = jnp.sum(
            jnp.where(matched, flat_weights[None, :], jnp.zeros((), jnp.float32)), axis=1
        )
        return (image_rows, weight_rows)

    image_blocks, weight_blocks = lax.map(sum_block, jnp.arange(pieces // sum_block_rows))
    weighted_sum = image_blocks.reshape(pieces, block_width)
    weight_sum = weight_blocks.reshape(pieces)
    coadd_image = weighted_sum / jnp.maximum(weight_sum, 1.0)[:, None]
    return (coadd_image[None], weight_sum[None])


def solution(mesh):
    in_specs = (
        P("expo", "fp", None),
        P(),
        P("expo", "fp"),
        P("expo", "fp"),
        P("expo", "fp"),
        P("expo", "fp", None, None),
        P("expo", "fp", None),
    )
    out_specs = (P(("expo", "fp"), None, None), P(("expo", "fp"), None))
    return jax.shard_map(body, mesh=mesh, in_specs=in_specs, out_specs=out_specs, check_vma=False)
```

profile of v0, /device:TPU:1, one launch (start us, length us, event | category | flops | bytes accessed | tf_op | source)
XLA Modules:
  0.0 234.6 jit_solution(11637574136949933219)
XLA Ops:
  1.6 4.9 %collective-permute-start = (bf16[1,20,2048]{2,1,0:T(8,128)(2,1)S(1)}, bf16[1,20,2048]{2,1,0:T(8,128)(2,1)S(1)}, u32[]{:S(2)}, u32[]{:S(2)}) collective-permute-start(bf16[1,20,2048]{2,1,0:T(8,128)(2,1)S(1)} %get-tuple-element.190), channel_id=1, source_target_pairs={{0,1},{1,2},{2,3},{3,4},{4,5},{5,6},{6,7},{7,8},{8,9},{9,10},{10,1... | collective-permute-start | bytes 245768 | tf_op jit(solution)/shard_map/ppermute | solution.py:18
  6.6 1.9 collective-permute-start.1
  26.5 66.3 %while.30 = (s32[]{:T(128)}, bf16[8,1,1024,128]{3,2,1,0:T(8,128)(2,1)}, s32[8,1,1024]{2,1,0:T(1,128)S(1)}, bf16[8,1,1024]{2,1,0:T(2,128)(2,1)S(1)}, s32[1,4096]{...) while((s32[]{:T(128)}, ...), condition=%wide.wide.region_6.7_spmd.clone, body=%wide.wide.region_3.6_spmd.clone.sunk | while | flops 1103232000 | bytes 1483941 | solution.py:109
  27.9 1.8 fusion.106
  30.0 1.8 fusion.107
  31.8 3.1 %fusion.105 = bf16[8,1,1024,128]{3,2,1,0:T(8,128)(2,1)} fusion(bf16[8,1,1024,128]{3,2,1,0:T(8,128)(2,1)} %get-tuple-element.384, s32[]{:T(128)S(6)} %copy.79, s32[4096]{0:T(1024)S(1)} %bitcast.200, s32[1024]{0:T(1024)S(1)} %iota_add_fusion.11, bf16[1,4096,128]{2,1,0:T(8,128)(2,1)S(1)} %get-tuple-element.401), kind=kOutput, calls=%fused_computation.21.clone.clone.1 | convolution fusion | flops 1078067200 | bytes 1331204 | tf_op jit(solution)/shard_map/while/body/eval_jaxpr/ebp,epc->ebc/dot_general | solution.py:97
  36.1 1.8 fusion.106
  38.2 1.8 fusion.107
  40.1 3.1 %fusion.105 = bf16[8,1,1024,128]{3,2,1,0:T(8,128)(2,1)} fusion(bf16[8,1,1024,128]{3,2,1,0:T(8,128)(2,1)} %get-tuple-element.384, s32[]{:T(128)S(6)} %copy.79, s32[4096]{0:T(1024)S(1)} %bitcast.200, s32[1024]{0:T(1024)S(1)} %iota_add_fusion.11, bf16[1,4096,128]{2,1,0:T(8,128)(2,1)S(1)} %get-tuple-element.401), kind=kOutput, calls=%fused_computation.21.clone.clone.1 | convolution fusion | flops 1078067200 | bytes 1331204 | tf_op jit(solution)/shard_map/while/body/eval_jaxpr/ebp,epc->ebc/dot_general | solution.py:97
  44.4 1.8 fusion.106
  46.5 1.8 fusion.107
  48.3 3.1 %fusion.105 = bf16[8,1,1024,128]{3,2,1,0:T(8,128)(2,1)} fusion(bf16[8,1,1024,128]{3,2,1,0:T(8,128)(2,1)} %get-tuple-element.384, s32[]{:T(128)S(6)} %copy.79, s32[4096]{0:T(1024)S(1)} %bitcast.200, s32[1024]{0:T(1024)S(1)} %iota_add_fusion.11, bf16[1,4096,128]{2,1,0:T(8,128)(2,1)S(1)} %get-tuple-element.401), kind=kOutput, calls=%fused_computation.21.clone.clone.1 | convolution fusion | flops 1078067200 | bytes 1331204 | tf_op jit(solution)/shard_map/while/body/eval_jaxpr/ebp,epc->ebc/dot_general | solution.py:97
  52.7 1.8 fusion.106
  54.7 1.8 fusion.107
  56.6 3.1 %fusion.105 = bf16[8,1,1024,128]{3,2,1,0:T(8,128)(2,1)} fusion(bf16[8,1,1024,128]{3,2,1,0:T(8,128)(2,1)} %get-tuple-element.384, s32[]{:T(128)S(6)} %copy.79, s32[4096]{0:T(1024)S(1)} %bitcast.200, s32[1024]{0:T(1024)S(1)} %iota_add_fusion.11, bf16[1,4096,128]{2,1,0:T(8,128)(2,1)S(1)} %get-tuple-element.401), kind=kOutput, calls=%fused_computation.21.clone.clone.1 | convolution fusion | flops 1078067200 | bytes 1331204 | tf_op jit(solution)/shard_map/while/body/eval_jaxpr/ebp,epc->ebc/dot_general | solution.py:97
  60.9 1.8 fusion.106
  63.0 1.8 fusion.107
  64.8 3.1 %fusion.105 = bf16[8,1,1024,128]{3,2,1,0:T(8,128)(2,1)} fusion(bf16[8,1,1024,128]{3,2,1,0:T(8,128)(2,1)} %get-tuple-element.384, s32[]{:T(128)S(6)} %copy.79, s32[4096]{0:T(1024)S(1)} %bitcast.200, s32[1024]{0:T(1024)S(1)} %iota_add_fusion.11, bf16[1,4096,128]{2,1,0:T(8,128)(2,1)S(1)} %get-tuple-element.401), kind=kOutput, calls=%fused_computation.21.clone.clone.1 | convolution fusion | flops 1078067200 | bytes 1331204 | tf_op jit(solution)/shard_map/while/body/eval_jaxpr/ebp,epc->ebc/dot_general | solution.py:97
  69.2 1.8 fusion.106
  71.3 1.8 fusion.107
  73.1 3.1 %fusion.105 = bf16[8,1,1024,128]{3,2,1,0:T(8,128)(2,1)} fusion(bf16[8,1,1024,128]{3,2,1,0:T(8,128)(2,1)} %get-tuple-element.384, s32[]{:T(128)S(6)} %copy.79, s32[4096]{0:T(1024)S(1)} %bitcast.200, s32[1024]{0:T(1024)S(1)} %iota_add_fusion.11, bf16[1,4096,128]{2,1,0:T(8,128)(2,1)S(1)} %get-tuple-element.401), kind=kOutput, calls=%fused_computation.21.clone.clone.1 | convolution fusion | flops 1078067200 | bytes 1331204 | tf_op jit(solution)/shard_map/while/body/eval_jaxpr/ebp,epc->ebc/dot_general | solution.py:97
  79.5 1.8 fusion.107
  81.4 3.1 %fusion.105 = bf16[8,1,1024,128]{3,2,1,0:T(8,128)(2,1)} fusion(bf16[8,1,1024,128]{3,2,1,0:T(8,128)(2,1)} %get-tuple-element.384, s32[]{:T(128)S(6)} %copy.79, s32[4096]{0:T(1024)S(1)} %bitcast.200, s32[1024]{0:T(1024)S(1)} %iota_add_fusion.11, bf16[1,4096,128]{2,1,0:T(8,128)(2,1)S(1)} %get-tuple-element.401), kind=kOutput, calls=%fused_computation.21.clone.clone.1 | convolution fusion | flops 1078067200 | bytes 1331204 | tf_op jit(solution)/shard_map/while/body/eval_jaxpr/ebp,epc->ebc/dot_general | solution.py:97
  89.7 3.1 %fusion.105 = bf16[8,1,1024,128]{3,2,1,0:T(8,128)(2,1)} fusion(bf16[8,1,1024,128]{3,2,1,0:T(8,128)(2,1)} %get-tuple-element.384, s32[]{:T(128)S(6)} %copy.79, s32[4096]{0:T(1024)S(1)} %bitcast.200, s32[1024]{0:T(1024)S(1)} %iota_add_fusion.11, bf16[1,4096,128]{2,1,0:T(8,128)(2,1)S(1)} %get-tuple-element.401), kind=kOutput, calls=%fused_computation.21.clone.clone.1 | convolution fusion | flops 1078067200 | bytes 1331204 | tf_op jit(solution)/shard_map/while/body/eval_jaxpr/ebp,epc->ebc/dot_general | solution.py:97
  93.6 10.2 %all-to-all-start.1 = ((bf16[128,1,64]{2,1,0:T(2,128)(2,1)}), bf16[128,1,64]{2,1,0:T(2,128)(2,1)S(1)}, u32[]{:S(2)}, u32[]{:S(2)}) async-start(bf16[128,1,64]{2,1,0:T(2,128)(2,1)} %convert_element_type.174), calls=%async_computation.1 | async-start | bytes 131072 | tf_op jit(solution)/shard_map/all_to_all | solution.py:125
  104.0 9.2 %all-to-all-done.1 = bf16[128,1,64]{2,1,0:T(2,128)(2,1)S(1)} async-done(((bf16[128,1,64]{2,1,0:T(2,128)(2,1)}), bf16[128,1,64]{2,1,0:T(2,128)(2,1)S(1)}, u32[]{:S(2)}, u32[]{:S(2)}) %all-to-all-start.1) | async-done | bytes 16416 | tf_op jit(solution)/shard_map/all_to_all | solution.py:125
  113.1 13.8 %all_to_all.15 = s32[128,1,64]{2,1,0:T(1,128)S(1)} all-to-all(s32[128,1,64]{2,1,0:T(1,128)S(1)} %bitcast.188), channel_id=1, replica_groups=mesh['expo'=4,'fp'=32] {'expo','fp'}, dimensions={0} | all-to-all | bytes 65536 | tf_op jit(solution)/shard_map/all_to_all | solution.py:124
  127.0 4.6 %all-to-all-start.2 = ((bf16[128,1,64,128]{3,2,1,0:T(8,128)(2,1)}), bf16[128,1,64,128]{3,2,1,0:T(8,128)(2,1)S(1)}, u32[]{:S(2)}, u32[]{:S(2)}) async-start(bf16[128,1,64,128]{3,2,1,0:T(8,128)(2,1)} %bitcast.181), calls=%async_computation.2 | async-start | bytes 4194304 | tf_op jit(solution)/shard_map/all_to_all | solution.py:123
  132.1 29.8 %all-to-all-done.2 = bf16[128,1,64,128]{3,2,1,0:T(8,128)(2,1)S(1)} async-done(((bf16[128,1,64,128]{3,2,1,0:T(8,128)(2,1)}), bf16[128,1,64,128]{3,2,1,0:T(8,128)(2,1)S(1)}, u32[]{:S(2)}, u32[]{:S(2)}) %all-to-all-start.2) | async-done | bytes 2097184 | tf_op jit(solution)/shard_map/all_to_all | solution.py:123
  162.0 3.5 %fusion.26 = (bf16[8192,128]{1,0:T(8,128)(2,1)S(1)}, bf16[8192,128]{1,0:T(8,128)(2,1)S(1)}) fusion(bf16[128,1,64,128]{3,2,1,0:T(8,128)(2,1)S(1)} %all-to-all-done.2, f32[8192]{0:T(1024)S(1)} %mul.46), kind=kLoop, calls=%fused_computation.29 | loop fusion | flops 6291456 | bytes 6324224 | tf_op jit(solution)/shard_map/convert_element_type | solution.py:137
  165.4 2.4 %pad_maximum_fusion = bf16[8192,256]{1,0:T(8,128)(2,1)} fusion(bf16[8192,128]{1,0:T(8,128)(2,1)S(1)} %get-tuple-element.189, bf16[8192,128]{1,0:T(8,128)(2,1)S(1)} %get-tuple-element.188), kind=kLoop, calls=%fused_computation.26 | loop fusion | flops 8388608 | bytes 8388608 | tf_op jit(solution)/shard_map/concatenate | solution.py:139
  167.8 64.5 %while.29 = (s32[]{:T(128)}, f32[8,512,128]{2,1,0:T(8,128)S(1)}, f32[8,512]{1,0:T(8,128)S(1)}, s32[8]{0:T(128)S(1)}, s32[128,1,64]{2,0,1:T(8,128)}, /*index=5*/b...) while((s32[]{:T(128)}, f32[8,512,128]{2,1,0:T(8,128)S(1)}, ...), condition=%wide.wide.region_9.10_spmd, body=%wide.wide.region_7.9_spmd.sunk | while | flops 2164326400 | bytes 5615777 | solution.py:154
  169.1 2.1 fusion.102
  171.3 4.6 %fusion.100 = f32[512,256]{1,0:T(8,128)S(1)} fusion(bf16[8192,256]{1,0:T(8,128)(2,1)} %get-tuple-element.436, s32[8192]{0:T(1024)S(1)} %get-tuple-element.438, s32[512]{0:T(512)S(1)} %iota_add_fusion.10), kind=kOutput, calls=%fused_computation.2.clone.clone.1 | convolution fusion | flops 2151677952 | bytes 4753408 | tf_op jit(solution)/shard_map/while/body/eval_jaxpr/dot_general | solution.py:145
  177.1 2.1 fusion.102
  179.3 4.6 %fusion.100 = f32[512,256]{1,0:T(8,128)S(1)} fusion(bf16[8192,256]{1,0:T(8,128)(2,1)} %get-tuple-element.436, s32[8192]{0:T(1024)S(1)} %get-tuple-element.438, s32[512]{0:T(512)S(1)} %iota_add_fusion.10), kind=kOutput, calls=%fused_computation.2.clone.clone.1 | convolution fusion | flops 2151677952 | bytes 4753408 | tf_op jit(solution)/shard_map/while/body/eval_jaxpr/dot_general | solution.py:145
  185.2 2.1 fusion.102
  187.4 4.6 %fusion.100 = f32[512,256]{1,0:T(8,128)S(1)} fusion(bf16[8192,256]{1,0:T(8,128)(2,1)} %get-tuple-element.436, s32[8192]{0:T(1024)S(1)} %get-tuple-element.438, s32[512]{0:T(512)S(1)} %iota_add_fusion.10), kind=kOutput, calls=%fused_computation.2.clone.clone.1 | convolution fusion | flops 2151677952 | bytes 4753408 | tf_op jit(solution)/shard_map/while/body/eval_jaxpr/dot_general | solution.py:145
  193.3 2.1 fusion.102
  195.5 4.6 %fusion.100 = f32[512,256]{1,0:T(8,128)S(1)} fusion(bf16[8192,256]{1,0:T(8,128)(2,1)} %get-tuple-element.436, s32[8192]{0:T(1024)S(1)} %get-tuple-element.438, s32[512]{0:T(512)S(1)} %iota_add_fusion.10), kind=kOutput, calls=%fused_computation.2.clone.clone.1 | convolution fusion | flops 2151677952 | bytes 4753408 | tf_op jit(solution)/shard_map/while/body/eval_jaxpr/dot_general | solution.py:145
  201.3 2.1 fusion.102
  203.5 4.6 %fusion.100 = f32[512,256]{1,0:T(8,128)S(1)} fusion(bf16[8192,256]{1,0:T(8,128)(2,1)} %get-tuple-element.436, s32[8192]{0:T(1024)S(1)} %get-tuple-element.438, s32[512]{0:T(512)S(1)} %iota_add_fusion.10), kind=kOutput, calls=%fused_computation.2.clone.clone.1 | convolution fusion | flops 2151677952 | bytes 4753408 | tf_op jit(solution)/shard_map/while/body/eval_jaxpr/dot_general | solution.py:145
  209.4 2.1 fusion.102
  211.6 4.6 %fusion.100 = f32[512,256]{1,0:T(8,128)S(1)} fusion(bf16[8192,256]{1,0:T(8,128)(2,1)} %get-tuple-element.436, s32[8192]{0:T(1024)S(1)} %get-tuple-element.438, s32[512]{0:T(512)S(1)} %iota_add_fusion.10), kind=kOutput, calls=%fused_computation.2.clone.clone.1 | convolution fusion | flops 2151677952 | bytes 4753408 | tf_op jit(solution)/shard_map/while/body/eval_jaxpr/dot_general | solution.py:145
  217.5 2.1 fusion.102
  219.6 4.6 %fusion.100 = f32[512,256]{1,0:T(8,128)S(1)} fusion(bf16[8192,256]{1,0:T(8,128)(2,1)} %get-tuple-element.436, s32[8192]{0:T(1024)S(1)} %get-tuple-element.438, s32[512]{0:T(512)S(1)} %iota_add_fusion.10), kind=kOutput, calls=%fused_computation.2.clone.clone.1 | convolution fusion | flops 2151677952 | bytes 4753408 | tf_op jit(solution)/shard_map/while/body/eval_jaxpr/dot_general | solution.py:145
  225.5 2.1 fusion.102
  227.7 4.6 %fusion.100 = f32[512,256]{1,0:T(8,128)S(1)} fusion(bf16[8192,256]{1,0:T(8,128)(2,1)} %get-tuple-element.436, s32[8192]{0:T(1024)S(1)} %get-tuple-element.438, s32[512]{0:T(512)S(1)} %iota_add_fusion.10), kind=kOutput, calls=%fused_computation.2.clone.clone.1 | convolution fusion | flops 2151677952 | bytes 4753408 | tf_op jit(solution)/shard_map/while/body/eval_jaxpr/dot_general | solution.py:145
  (164 shorter events, 37.9 us)
Async XLA Ops:
  0.6 11.4 %copy-start = (bf16[8,2,41]{2,1,0:T(2,128)(2,1)S(1)}, bf16[8,2,41]{2,1,0:T(2,128)(2,1)}, u32[]{:S(2)}) copy-start(bf16[8,2,41]{2,1,0:T(2,128)(2,1)} %param.12) | copy-start | bytes 3940
  1.6 21.1 %collective-permute-start = (bf16[1,20,2048]{2,1,0:T(8,128)(2,1)S(1)}, bf16[1,20,2048]{2,1,0:T(8,128)(2,1)S(1)}, u32[]{:S(2)}, u32[]{:S(2)}) collective-permute-start(bf16[1,20,2048]{2,1,0:T(8,128)(2,1)S(1)} %get-tuple-element.190), channel_id=1, source_target_pairs={{0,1},{1,2},{2,3},{3,4},{4,5},{5,6},{6,7},{7,8},{8,9},{9,10},{10,1... | collective-permute-start | bytes 245768 | tf_op jit(solution)/shard_map/ppermute | solution.py:18
  6.6 16.2 %collective-permute-start.1 = (bf16[1,20,2048]{2,1,0:T(8,128)(2,1)S(1)}, bf16[1,20,2048]{2,1,0:T(8,128)(2,1)S(1)}, u32[]{:S(2)}, u32[]{:S(2)}) collective-permute-start(bf16[1,20,2048]{2,1,0:T(8,128)(2,1)S(1)} %get-tuple-element.191), channel_id=1, source_target_pairs={{1,0},{2,1},{3,2},{4,3},{5,4},{6,5},{7,6},{8,7},{9,8},{10,9},{11,1... | collective-permute-start | bytes 245768 | tf_op jit(solution)/shard_map/ppermute | solution.py:19
  13.6 3.0 %copy-start.3 = (s32[1,256,16]{2,1,0:T(8,128)}, s32[1,256,16]{2,1,0:T(8,128)S(1)}, u32[]{:S(2)}) copy-start(s32[1,256,16]{2,1,0:T(8,128)S(1)} %copy.35) | copy-start | bytes 49156
  20.2 2.6 %copy-start.2 = (bf16[1,256,2048]{2,1,0:T(8,128)(2,1)S(1)}, bf16[1,256,2048]{2,1,0:T(8,128)(2,1)}, u32[]{:S(2)}) copy-start(bf16[1,256,2048]{2,1,0:T(8,128)(2,1)} %param.11) | copy-start | bytes 3145732
  93.6 19.5 %all-to-all-start.1 = ((bf16[128,1,64]{2,1,0:T(2,128)(2,1)}), bf16[128,1,64]{2,1,0:T(2,128)(2,1)S(1)}, u32[]{:S(2)}, u32[]{:S(2)}) async-start(bf16[128,1,64]{2,1,0:T(2,128)(2,1)} %convert_element_type.174), calls=%async_computation.1 | async-start | bytes 131072 | tf_op jit(solution)/shard_map/all_to_all | solution.py:125
  127.0 5.1 %copy-start.4 = (s32[128,1,64]{2,1,0:T(1,128)}, s32[128,1,64]{2,1,0:T(1,128)S(1)}, u32[]{:S(2)}) copy-start(s32[128,1,64]{2,1,0:T(1,128)S(1)} %all_to_all.15) | copy-start | bytes 98308
  127.0 35.0 %all-to-all-start.2 = ((bf16[128,1,64,128]{3,2,1,0:T(8,128)(2,1)}), bf16[128,1,64,128]{3,2,1,0:T(8,128)(2,1)S(1)}, u32[]{:S(2)}, u32[]{:S(2)}) async-start(bf16[128,1,64,128]{3,2,1,0:T(8,128)(2,1)} %bitcast.181), calls=%async_computation.2 | async-start | bytes 4194304 | tf_op jit(solution)/shard_map/all_to_all | solution.py:123
  132.0 33.5 %copy-start.5 = (f32[128,1,64]{2,1,0:T(1,128)}, f32[128,1,64]{2,1,0:T(1,128)S(1)}, u32[]{:S(2)}) copy-start(f32[128,1,64]{2,1,0:T(1,128)S(1)} %convert_element_type.166) | copy-start | bytes 98308
  165.4 2.4 %copy-start.1 = (f32[8,512,128]{2,1,0:T(8,128)S(1)}, f32[8,512,128]{2,1,0:T(8,128)}, u32[]{:S(2)}) copy-start(f32[8,512,128]{2,1,0:T(8,128)} %custom-call) | copy-start | bytes 6291460
where the time goes:
time: 236 us; the launch traced here: 235 us
  matrix products  69.9 us (30%)
  other arithmetic  58.4 us (25%)
  waiting for transfers between devices  39 us (17%)
  starting transfers between devices  21.7 us (9%)
  local copies, waits for them, and re-layouts  17.8 us (8%)
  blocking collectives  13.8 us (6%)
  loops' own time  11 us (5%)
  between operations  3.02 us (1%)
    dot_general x8, matrix products, sum_block(): jnp.dot(matched.astype(jnp.bfloat16), both_parts, preferred_element_type=...  36.5 us
    all_to_all x1, waiting for transfers between devices, body(): lax.all_to_all(send_values, ('expo', 'fp'), split_axis=0, concat_axis=0,...  29.8 us
    dot_general x8, matrix products, pack_block(): jnp.einsum('ebp,epc->ebc', matched.astype(jnp.bfloat16), convolved, prefe...  24.9 us
    reduce_sum x8, other arithmetic, sum_block(): jnp.sum(jnp.where(matched, flat_weights[None, :], jnp.zeros((), jnp.float...  16.9 us
    reduce_sum x8, other arithmetic, pack_block(): slot_offsets = jnp.sum(jnp.where(matched, offsets[:, None, :], 0), axis=2)  14.7 us
    reduce_sum x8, other arithmetic, pack_block(): jnp.sum(jnp.where(matched, piece_weight[:, None, :], jnp.zeros((), jnp.fl...  14.7 us
    all_to_all x1, blocking collectives, body(): lax.all_to_all(send_offsets, ('expo', 'fp'), split_axis=0, concat_axis=0,...  13.8 us
    all_to_all x1, starting transfers between devices, body(): lax.all_to_all(send_weights.astype(jnp.bfloat16), ('expo', 'fp'), split_a...  10.2 us
  transfers between devices with their start and end apart: 4, of which 2 were waited for; matrix products, arithmetic and copies ran while one was open for 5% of the time, Pallas kernels for 0%

commit v1 on v0

v1 whole, which is shorter than its diff:
```python
import jax
import jax.numpy as jnp
from jax import lax
from jax.experimental import pallas as pl
from jax.experimental.pallas import tpu as pltpu
from jax.sharding import PartitionSpec as P

GAP = 32
SEG = 128
CAP = 64
HALO = 32
FP = 32
DEVICES = 128
MESH = pl.DeviceIdType.MESH
NT = (((1,), (1,)), ((), ()))


def target(step):
    y = lax.axis_index("expo")
    f = lax.axis_index("fp")
    a, b, c = lax.rem(step // 2, 4), lax.rem(step // 8, 4), step // 32
    ty = lax.rem(y + a + c, 4)
    tx = lax.rem(f // 8 + a + b, 4)
    tz = lax.rem(lax.rem(f // 2, 4) + a + b + c, 4)
    tc = lax.rem(f + step, 2)
    return ty, tx * 8 + tz * 2 + tc


def route_kernel(inv_ref, gap_ref, tile_ref, off_ref, src_ref, meta_ref):
    segs, rows = tile_ref.shape
    inv = inv_ref[0, 0]
    gap = gap_ref[0, 0]
    before = lax.broadcasted_iota(jnp.int32, (rows, rows), 0)
    after = lax.broadcasted_iota(jnp.int32, (rows, rows), 1)
    upper = (before < after).astype(jnp.float32).astype(jnp.bfloat16)
    tile_iota = lax.broadcasted_iota(jnp.int32, (DEVICES, rows), 0)
    slot_iota = lax.broadcasted_iota(jnp.int32, (CAP, rows), 0)
    row = lax.broadcasted_iota(jnp.int32, (1, rows), 1)
    open_row = jnp.where((row >= gap) & (row < gap + GAP), 0.0, 1.0)
    row_f = row.astype(jnp.float32)
    base = jnp.zeros((DEVICES, 1), jnp.float32)
    found = jnp.zeros((DEVICES, 5 * CAP), jnp.float32)
    for s in range(segs):
        hot = (tile_iota == tile_ref[s : s + 1, :]).astype(jnp.float32)
        hot_b = hot.astype(jnp.bfloat16)
        inside = jnp.dot(hot_b, upper, preferred_element_type=jnp.float32)
        rank = jnp.sum(hot * (inside + base), axis=0, keepdims=True)
        base = base + jnp.sum(hot, axis=1, keepdims=True)
        at_slot = (slot_iota == rank.astype(jnp.int32)).astype(jnp.float32)
        offset = off_ref[s : s + 1, :] + 1
        packed = jnp.concatenate(
            [
                at_slot * float(s),
                at_slot * row_f,
                at_slot * (offset >> 6).astype(jnp.float32),
                at_slot * (offset & 63).astype(jnp.float32),
                at_slot * open_row,
            ],
            axis=0,
        ).astype(jnp.bfloat16)
        found = found + lax.dot_general(hot_b, packed, NT, preferred_element_type=jnp.float32)
    source = found[:, :CAP] * float(rows) + found[:, CAP : 2 * CAP]
    src_ref[...] = source.astype(jnp.int32)
    offset = found[:, 2 * CAP : 3 * CAP] * 64.0 + found[:, 3 * CAP : 4 * CAP] - 1.0
    meta_ref[:, 0, :] = jnp.concatenate([offset, found[:, 4 * CAP :] * inv], axis=1)


def band(taps, rows, width, shift):
    wide = jnp.broadcast_to(taps[:, :width], (rows, width))
    return pltpu.roll(wide, shift - 4, 1, stride=1, stride_axis=0).astype(jnp.bfloat16)


def conv_kernel(
    id_ref, inv_ref, gap_ref, src_ref, bank_ref, up_ref, raw_ref, down_ref, send_ref,
    framed, vertical, pieces, stage,
):
    rows, cols = raw_ref.shape
    half = SEG
    kernel_id = id_ref[0, 0]
    vtap = bank_ref[pl.ds(2 * kernel_id, 1), :]
    htap = bank_ref[pl.ds(2 * kernel_id + 1, 1), :]
    framed[0:32, :] = jnp.zeros((32, cols), jnp.bfloat16)
    framed[32:64, :] = up_ref[...]
    framed[64 : 64 + rows, :] = raw_ref[...]
    framed[64 + rows : 96 + rows, :] = down_ref[...]
    framed[96 + rows : 128 + rows, :] = jnp.zeros((32, cols), jnp.bfloat16)
    vertical[:, :SEG] = jnp.zeros((rows, SEG), jnp.bfloat16)
    vertical[:, SEG + cols :] = jnp.zeros((rows, SEG), jnp.bfloat16)
    vband = band(vtap, half, 256, 44)
    hband = band(htap, 256, 512, 108)
    for n in range(cols // 512):
        for m in range(rows // half):
            made = jnp.dot(
                vband,
                framed[m * half : m * half + 256, n * 512 : (n + 1) * 512],
                preferred_element_type=jnp.float32,
            )
            vertical[m * half : (m + 1) * half, SEG + n * 512 : SEG + (n + 1) * 512] = made.astype(
                jnp.bfloat16
            )
    row = lax.broadcasted_iota(jnp.int32, (rows, 256), 0)
    gap = gap_ref[0, 0]
    weight = jnp.where((row >= gap) & (row < gap + GAP), 0.0, inv_ref[0, 0])
    for n in range(cols // 256):
        made = lax.dot_general(
            vertical[:, n * 256 : n * 256 + 512], hband, NT, preferred_element_type=jnp.float32
        )
        made = made.astype(jnp.bfloat16).astype(jnp.float32) * weight
        pieces[2 * n * rows : (2 * n + 1) * rows, :] = made[:, :SEG]
        pieces[(2 * n + 1) * rows : (2 * n + 2) * rows, :] = made[:, SEG:]

    def pack(pair, carry):
        for side in range(2):
            for k in range(CAP):
                stage[side, k : k + 1, :] = pieces[pl.ds(src_ref[2 * pair + side, k], 1), :]
        for side in range(2):
            send_ref[2 * pair + side] = stage[side].astype(jnp.bfloat16)
        return carry

    lax.fori_loop(0, DEVICES // 2, pack, 0)


def exchange_kernel(send_ref, meta_ref, got_ref, gmeta_ref, vsend, vrecv, msend, mrecv, local):
    barrier = pltpu.get_barrier_semaphore()

    def greet(step, carry):
        pl.semaphore_signal(barrier, inc=1, device_id=target(step), device_id_type=MESH)
        return carry

    lax.fori_loop(1, DEVICES, greet, 0)
    me = lax.axis_index("expo") * FP + lax.axis_index("fp")
    own = pltpu.make_async_copy(send_ref.at[me], got_ref.at[0], local.at[0])
    own.start()
    own_meta = pltpu.make_async_copy(meta_ref.at[me], gmeta_ref.at[0], local.at[1])
    own_meta.start()
    pl.semaphore_wait(barrier, DEVICES - 1)

    def copies(step):
        ty, tf = target(step)
        to = ty * FP + tf
        return (
            pltpu.make_async_remote_copy(
                src_ref=meta_ref.at[to], dst_ref=gmeta_ref.at[step],
                send_sem=msend.at[step], recv_sem=mrecv.at[step],
                device_id=(ty, tf), device_id_type=MESH,
            ),
            pltpu.make_async_remote_copy(
                src_ref=send_ref.at[to], dst_ref=got_ref.at[step],
                send_sem=vsend.at[step], recv_sem=vrecv.at[step],
                device_id=(ty, tf), device_id_type=MESH,
            ),
        )

    def start(step, carry):
        for copy in copies(step):
            copy.start()
        return carry

    def finish(step, carry):
        for copy in copies(step):
            copy.wait()
        return carry

    lax.fori_loop(1, DEVICES, start, 0)
    lax.fori_loop(1, DEVICES, finish, 0)
    own.wait()
    own_meta.wait()


PARTS = 8
SPAN = 512
GROUP = 8


def coadd_kernel(got_ref, gmeta_ref, image_ref, weight_ref, total):
    span_iota = lax.broadcasted_iota(jnp.int32, (SPAN, GROUP * CAP), 0)
    lane = lax.broadcasted_iota(jnp.int32, (GROUP * CAP, SEG), 1)
    total[...] = jnp.zeros_like(total)

    def chunk(j, carry):
        meta = gmeta_ref[pl.ds(j * GROUP, GROUP), 0, :]
        slots = jnp.concatenate([meta[i : i + 1, :CAP] for i in range(GROUP)], axis=1)
        slots = slots.astype(jnp.int32) & (SPAN - 1)
        hot = (span_iota == slots).astype(jnp.float32).astype(jnp.bfloat16)
        turned = meta.T
        column = jnp.concatenate([turned[:CAP, i : i + 1] for i in range(GROUP)], axis=0)
        part = jnp.broadcast_to(column, (GROUP * CAP, SEG)).astype(jnp.int32) >> 9
        weight = jnp.concatenate([turned[CAP:, i : i + 1] for i in range(GROUP)], axis=0)
        weight = jnp.broadcast_to(weight, (GROUP * CAP, SEG))
        high = weight.astype(jnp.bfloat16).astype(jnp.float32)
        spread = jnp.where(lane == part, high, 0.0)
        spread = spread + jnp.where(lane == part + PARTS, jnp.where(part < 0, 0.0, weight - high), 0.0)
        values = got_ref[pl.ds(j * GROUP, GROUP)].reshape(GROUP * CAP, SEG)
        values = values.astype(jnp.float32)
        masked = [jnp.where(part == a, values, 0.0).astype(jnp.bfloat16) for a in range(PARTS)]
        right = jnp.concatenate(masked + [spread.astype(jnp.bfloat16)], axis=1)
        total[...] += jnp.dot(hot, right, preferred_element_type=jnp.float32)
        return carry

    lax.fori_loop(0, DEVICES // GROUP, chunk, 0)
    sums = total[:, PARTS * SEG :]
    sums = sums[:, :PARTS] + sums[:, PARTS : 2 * PARTS]
    for a in range(PARTS):
        divisor = jnp.maximum(sums[:, a : a + 1], 1.0)
        image_ref[a * SPAN : (a + 1) * SPAN, :] = total[:, a * SEG : (a + 1) * SEG] / divisor
    turned = sums.T
    for a in range(PARTS):
        weight_ref[:, a * SPAN : (a + 1) * SPAN] = turned[a : a + 1, :]


def body(raw_pixels, kernel_bank, kernel_ids, inv_var, gap_start, warp_tile, warp_offset):
    raw = raw_pixels[0]
    rows, cols = raw.shape
    up = [(i, i + 1) for i in range(FP - 1)]
    down = [(i + 1, i) for i in range(FP - 1)]
    above = lax.ppermute(raw[rows - HALO :], "fp", up)
    below = lax.ppermute(raw[:HALO], "fp", down)
    bank = kernel_bank.astype(jnp.float32).reshape(-1, kernel_bank.shape[2])
    bank = jnp.pad(bank, ((0, 0), (4, 508 - bank.shape[1])))
    tiles = warp_tile[0, :, :, 0].T
    offsets = warp_offset[0].T
    smem = pl.BlockSpec(memory_space=pltpu.SMEM)
    vmem = pl.BlockSpec(memory_space=pltpu.VMEM)
    hbm = pl.BlockSpec(memory_space=pl.ANY)
    source, meta = pl.pallas_call(
        route_kernel,
        out_shape=(
            jax.ShapeDtypeStruct((DEVICES, CAP), jnp.int32),
            jax.ShapeDtypeStruct((DEVICES, 1, 2 * CAP), jnp.float32),
        ),
        in_specs=[smem, smem, vmem, vmem],
        out_specs=(vmem, vmem),
        cost_estimate=pl.CostEstimate(flops=10**9, bytes_accessed=10**6, transcendentals=0),
        name="route",
    )(inv_var, gap_start, tiles, offsets)
    send = pl.pallas_call(
        conv_kernel,
        out_shape=jax.ShapeDtypeStruct((DEVICES, CAP, SEG), jnp.bfloat16),
        in_specs=[smem, smem, smem, smem, vmem, vmem, vmem, vmem],
        out_specs=vmem,
        scratch_shapes=[
            pltpu.VMEM((rows + 128, cols), jnp.bfloat16),
            pltpu.VMEM((rows, cols + 2 * SEG), jnp.bfloat16),
            pltpu.VMEM((rows * cols // SEG, SEG), jnp.float32),
            pltpu.VMEM((2, CAP, SEG), jnp.float32),
        ],
        compiler_params=pltpu.CompilerParams(vmem_limit_bytes=40 << 20),
        name="conv_pack",
    )(kernel_ids, inv_var, gap_start, source, bank, above, raw, below)
    got, gmeta = pl.pallas_call(
        exchange_kernel,
        out_shape=(
            jax.ShapeDtypeStruct(send.shape, send.dtype),
            jax.ShapeDtypeStruct(meta.shape, meta.dtype),
        ),
        in_specs=[hbm, hbm],
        out_specs=(hbm, hbm),
        scratch_shapes=[pltpu.SemaphoreType.DMA((DEVICES,))] * 4 + [pltpu.SemaphoreType.DMA((2,))],
        compiler_params=pltpu.CompilerParams(collective_id=0, has_side_effects=True),
        name="exchange",
    )(send, meta)
    image, weight = pl.pallas_call(
        coadd_kernel,
        out_shape=(
            jax.ShapeDtypeStruct((PARTS * SPAN, SEG), jnp.float32),
            jax.ShapeDtypeStruct((1, PARTS * SPAN), jnp.float32),
        ),
        in_specs=[vmem, vmem],
        out_specs=(vmem, vmem),
        scratch_shapes=[pltpu.VMEM((SPAN, (PARTS + 1) * SEG), jnp.float32)],
        compiler_params=pltpu.CompilerParams(vmem_limit_bytes=40 << 20),
        name="coadd",
    )(got, gmeta)
    return image[None], weight


def solution(mesh):
    in_specs = (
        P("expo", "fp", None),
        P(),
        P("expo", "fp"),
        P("expo", "fp"),
        P("expo", "fp"),
        P("expo", "fp", None, None),
        P("expo", "fp", None),
    )
    out_specs = (P(("expo", "fp"), None, None), P(("expo", "fp"), None))
    return jax.shard_map(body, mesh=mesh, in_specs=in_specs, out_specs=out_specs, check_vma=False)
```

time: 236 us -> 99.9 us (0.42)
  Pallas kernels: 0 us -> 82.6 us
  matrix products: 69.9 us -> 0 us
  other arithmetic: 58.4 us -> 0.08 us
  waiting for transfers between devices: 39 us -> 0.01 us
  starting transfers between devices: 21.7 us -> 6.86 us
  blocking collectives: 13.8 us -> 0 us
  loops' own time: 11 us -> 0 us
  local copies, waits for them, and re-layouts: 17.8 us -> 6.98 us
    pallas_call x0 -> x4, Pallas kernels: none -> 82.6 us  [the longest x1 46.7 us: body(): pl.pallas_call(exchange_kernel, out_shape=(jax.ShapeDtypeStruct(send.shap...]
    dot_general x28 -> x0, matrix products: 69.9 us -> none  [the longest x8 36.5 us: sum_block(): jnp.dot(matched.astype(jnp.bfloat16), both_parts, preferred_element_type=...]
    reduce_sum x25 -> x0, other arithmetic: 46.8 us -> none  [the longest x8 16.9 us: sum_block(): jnp.sum(jnp.where(matched, flat_weights[None, :], jnp.zeros((), jnp.float...]
    all_to_all x2 -> x0, waiting for transfers between devices: 39 us -> none  [the longest x1 29.8 us: body(): lax.all_to_all(send_values, ('expo', 'fp'), split_axis=0, concat_axis=0,...]
    all_to_all x2 -> x0, starting transfers between devices: 14.8 us -> none  [the longest x1 10.2 us: body(): lax.all_to_all(send_weights.astype(jnp.bfloat16), ('expo', 'fp'), split_a...]
    all_to_all x1 -> x0, blocking collectives: 13.8 us -> none  [body(): lax.all_to_all(send_offsets, ('expo', 'fp'), split_axis=0, concat_axis=0,...]
    another operation x2 -> x0, loops' own time: 11 us -> none  [the longest x1 5.57 us: body(): lax.map(sum_block, jnp.arange(pieces // sum_block_rows))]
    dynamic_slice x16 -> x0, local copies, waits for them, and re-layouts: 9.41 us -> none  [body(): lax.map(pack_block, jnp.arange(send_slots // send_block))]
  transfers between devices with their start and end apart: 4 -> 2, of which waited for: 2 -> 0; matrix products, arithmetic and copies ran while one was open for 5% -> 1% of each run, Pallas kernels for 0% -> 5%
where the time goes in v1:
time: 99.9 us; the launch traced here: 99.1 us
  Pallas kernels  82.6 us (83%)
  local copies, waits for them, and re-layouts  6.98 us (7%)
  starting transfers between devices  6.86 us (7%)
  between operations  2.66 us (3%)
    pallas_call x1, Pallas kernels, body(): pl.pallas_call(exchange_kernel, out_shape=(jax.ShapeDtypeStruct(send.shap...  46.7 us
    pallas_call x1, Pallas kernels, body(): pl.pallas_call(coadd_kernel, out_shape=(jax.ShapeDtypeStruct((PARTS * SPA...  20.3 us
    pallas_call x1, Pallas kernels, body(): pl.pallas_call(conv_kernel, out_shape=jax.ShapeDtypeStruct((DEVICES, CAP,...  10.4 us
    unnamed x13, local copies, waits for them, and re-layouts  5.9 us
    pallas_call x1, Pallas kernels, body(): pl.pallas_call(route_kernel, out_shape=(jax.ShapeDtypeStruct((DEVICES, CA...  5.1 us
    ppermute x1, starting transfers between devices, body(): above = lax.ppermute(raw[rows - HALO:], 'fp', up)  3.53 us
    ppermute x1, starting transfers between devices, body(): below = lax.ppermute(raw[:HALO], 'fp', down)  3.33 us
  transfers between devices with their start and end apart: 2, of which 0 were waited for; matrix products, arithmetic and copies ran while one was open for 1% of the time, Pallas kernels for 5%

profile of v1, /device:TPU:1, one launch (start us, length us, event | category | flops | bytes accessed | tf_op | source)
XLA Modules:
  0.0 99.1 jit_solution(346076061186382244)
XLA Ops:
  0.6 0.0 copy-start.2
  0.6 0.0 copy-start.5
  0.6 1.1 %slice_bitcast_fusion = (bf16[32,2048]{1,0:T(8,128)(2,1)S(1)}, bf16[32,2048]{1,0:T(8,128)(2,1)S(1)}) fusion(bf16[1,256,2048]{2,1,0:T(8,128)(2,1)} %param.7), kind=kLoop, calls=%fused_computation | loop fusion | bytes 524288 | tf_op jit(solution)/shard_map/slice | solution.py:217
  1.7 3.3 %collective-permute-start.1 = (bf16[32,2048]{1,0:T(8,128)(2,1)S(1)}, bf16[32,2048]{1,0:T(8,128)(2,1)S(1)}, u32[]{:S(2)}, u32[]{:S(2)}) collective-permute-start(bf16[32,2048]{1,0:T(8,128)(2,1)S(1)} %get-tuple-element.14), channel_id=1, source_target_pairs={{1,0},{2,1},{3,2},{4,3},{5,4},{6,5},{7,6},{8,7},{9,8},{10,9},{11,1... | collective-permute-start | bytes 393224 | tf_op jit(solution)/shard_map/ppermute | solution.py:217
  5.1 3.5 %collective-permute-start = (bf16[32,2048]{1,0:T(8,128)(2,1)S(1)}, bf16[32,2048]{1,0:T(8,128)(2,1)S(1)}, u32[]{:S(2)}, u32[]{:S(2)}) collective-permute-start(bf16[32,2048]{1,0:T(8,128)(2,1)S(1)} %get-tuple-element.15), channel_id=1, source_target_pairs={{0,1},{1,2},{2,3},{3,4},{4,5},{5,6},{6,7},{7,8},{8,9},{9,10},{10,1... | collective-permute-start | bytes 393224 | tf_op jit(solution)/shard_map/ppermute | solution.py:216
  9.9 1.3 %copy.11 = s32[1,256,16,1]{1,2,3,0:T(8,128)} copy(s32[1,256,16,1]{1,3,2,0:T(1,128)} %param.12) | data formatting | bytes 32768
  11.2 5.1 %route.1 = (s32[128,64]{1,0:T(8,128)}, f32[128,1,128]{2,1,0:T(1,128)}) custom-call(f32[1,1]{1,0:T(1,128)S(6)} %copy.13.inv_ref, s32[1,1]{1,0:T(1,128)S(6)} %copy.14.gap_ref, s32[16,256]{1,0:T(8,128)} %bitcast.16, s32[16,256]{1,0:T(8,128)} %bitcast.19), custom_call_target="tpu_custom_call" | custom-call | flops 1000000000 | bytes 1000000 | tf_op jit(solution)/shard_map/route/pallas_call | solution.py:225
  17.0 0.0 copy-done.5
  17.0 0.1 pad_convert_fusion.bank_ref
  17.1 0.0 collective-permute-done.1.down_ref
  17.1 0.0 collective-permute-done.up_ref
  17.1 0.0 copy-done.2
  17.1 0.0 copy-start.3
  17.1 0.8 copy-done.3
  17.9 10.4 %conv_pack.1.send_ref = bf16[128,64,128]{2,1,0:T(8,128)(2,1)S(1)} custom-call(s32[1,1]{1,0:T(1,128)S(6)} %copy.12.id_ref, f32[1,1]{1,0:T(1,128)S(6)} %copy.13.inv_ref, s32[1,1]{1,0:T(1,128)S(6)} %copy.14.gap_ref, s32[128,64]{1,0:T(8,128)S(1)} %copy-done.3, f32[16,512]{1,0:T(8,128)S(1)} %pad_convert_fusion.bank_ref, ...), custom_call_target="tpu_custom_call" | custom-call | tf_op jit(solution)/shard_map/conv_pack/pallas_call | solution.py:236
  28.3 0.0 copy-start
  28.3 1.3 %copy-done = bf16[128,64,128]{2,1,0:T(8,128)(2,1)} copy-done((bf16[128,64,128]{2,1,0:T(8,128)(2,1)}, bf16[128,64,128]{2,1,0:T(8,128)(2,1)S(1)}, u32[]{:S(2)}) %copy-start) | copy-done | bytes 2097176
  29.6 46.7 %exchange.1 = (bf16[128,64,128]{2,1,0:T(8,128)(2,1)}, f32[128,1,128]{2,1,0:T(1,128)}) custom-call(bf16[128,64,128]{2,1,0:T(8,128)(2,1)} %copy-done, f32[128,1,128]{2,1,0:T(1,128)} %get-tuple-element.9.meta_ref), custom_call_target="tpu_custom_call" | custom-call | tf_op jit(solution)/shard_map/exchange/pallas_call | solution.py:250
  76.4 0.0 copy-start.1
  76.4 1.6 %copy-done.1 = bf16[128,64,128]{2,1,0:T(8,128)(2,1)S(1)} copy-done((bf16[128,64,128]{2,1,0:T(8,128)(2,1)S(1)}, bf16[128,64,128]{2,1,0:T(8,128)(2,1)}, u32[]{:S(2)}) %copy-start.1) | copy-done | bytes 2097176
  78.0 0.0 copy-start.4
  78.0 0.8 copy-done.4
  78.8 20.3 %coadd.1 = (f32[4096,128]{1,0:T(8,128)}, f32[1,4096]{1,0:T(1,128)}) custom-call(bf16[128,64,128]{2,1,0:T(8,128)(2,1)S(1)} %copy-done.1, f32[128,1,128]{2,1,0:T(1,128)S(1)} %copy-done.4), custom_call_target="tpu_custom_call" | custom-call | tf_op jit(solution)/shard_map/coadd/pallas_call | solution.py:262
Async XLA Ops:
  0.6 16.4 %copy-start.2 = (bf16[1,256,2048]{2,1,0:T(8,128)(2,1)S(1)}, bf16[1,256,2048]{2,1,0:T(8,128)(2,1)}, u32[]{:S(2)}) copy-start(bf16[1,256,2048]{2,1,0:T(8,128)(2,1)} %param.7) | copy-start | bytes 3145732
  0.6 16.3 %copy-start.5 = (bf16[8,2,41]{2,1,0:T(2,128)(2,1)S(1)}, bf16[8,2,41]{2,1,0:T(2,128)(2,1)}, u32[]{:S(2)}) copy-start(bf16[8,2,41]{2,1,0:T(2,128)(2,1)} %param.8) | copy-start | bytes 3940
  1.7 15.3 %collective-permute-start.1 = (bf16[32,2048]{1,0:T(8,128)(2,1)S(1)}, bf16[32,2048]{1,0:T(8,128)(2,1)S(1)}, u32[]{:S(2)}, u32[]{:S(2)}) collective-permute-start(bf16[32,2048]{1,0:T(8,128)(2,1)S(1)} %get-tuple-element.14), channel_id=1, source_target_pairs={{1,0},{2,1},{3,2},{4,3},{5,4},{6,5},{7,6},{8,7},{9,8},{10,9},{11,1... | collective-permute-start | bytes 393224 | tf_op jit(solution)/shard_map/ppermute | solution.py:217
  5.1 12.0 %collective-permute-start = (bf16[32,2048]{1,0:T(8,128)(2,1)S(1)}, bf16[32,2048]{1,0:T(8,128)(2,1)S(1)}, u32[]{:S(2)}, u32[]{:S(2)}) collective-permute-start(bf16[32,2048]{1,0:T(8,128)(2,1)S(1)} %get-tuple-element.15), channel_id=1, source_target_pairs={{0,1},{1,2},{2,3},{3,4},{4,5},{5,6},{6,7},{7,8},{8,9},{9,10},{10,1... | collective-permute-start | bytes 393224 | tf_op jit(solution)/shard_map/ppermute | solution.py:216
  17.1 0.8 copy-start.3
  28.3 1.3 %copy-start = (bf16[128,64,128]{2,1,0:T(8,128)(2,1)}, bf16[128,64,128]{2,1,0:T(8,128)(2,1)S(1)}, u32[]{:S(2)}) copy-start(bf16[128,64,128]{2,1,0:T(8,128)(2,1)S(1)} %conv_pack.1.send_ref) | copy-start | bytes 6291460
  76.4 1.6 %copy-start.1 = (bf16[128,64,128]{2,1,0:T(8,128)(2,1)S(1)}, bf16[128,64,128]{2,1,0:T(8,128)(2,1)}, u32[]{:S(2)}) copy-start(bf16[128,64,128]{2,1,0:T(8,128)(2,1)} %get-tuple-element.10.got_ref) | copy-start | bytes 6291460
  78.0 0.8 copy-start.4

commit v2 on v1

v2 whole, which is shorter than its diff:
```python
import jax
import jax.numpy as jnp
from jax import lax
from jax.experimental import pallas as pl
from jax.experimental.pallas import tpu as pltpu
from jax.sharding import PartitionSpec as P

GAP = 32
SEG = 128
CAP = 64
HALO = 32
FP = 32
DEVICES = 128
MESH = pl.DeviceIdType.MESH
NT = (((1,), (1,)), ((), ()))


def corner(group):
    y = lax.axis_index("expo")
    f = lax.axis_index("fp")
    b, c = lax.rem(group, 4), group // 4
    return y + c, f // 8 + b, lax.rem(f // 2, 4) + b + c, lax.rem(f, 2)


def target(at, i):
    y, x, z, core = at
    a = i // 2
    ty = lax.rem(y + a, 4)
    tf = lax.rem(x + a, 4) * 8 + lax.rem(z + a, 4) * 2 + lax.rem(core + i, 2)
    return ty, tf


def front_kernel(
    id_ref, inv_ref, gap_ref, bank_ref, tile_ref, off_ref, raw_ref,
    src_ref, meta_ref, taps_ref, up_ref, down_ref, send_sem, recv_sem,
):
    y = lax.axis_index("expo")
    f = lax.axis_index("fp")
    top = raw_ref.shape[0] - HALO
    barrier = pltpu.get_barrier_semaphore()
    to_next = pltpu.make_async_remote_copy(
        src_ref=raw_ref.at[pl.ds(top, HALO)], dst_ref=up_ref,
        send_sem=send_sem.at[0], recv_sem=recv_sem.at[0],
        device_id=(y, f + 1), device_id_type=MESH,
    )
    to_last = pltpu.make_async_remote_copy(
        src_ref=raw_ref.at[pl.ds(0, HALO)], dst_ref=down_ref,
        send_sem=send_sem.at[1], recv_sem=recv_sem.at[1],
        device_id=(y, f - 1), device_id_type=MESH,
    )

    @pl.when(f > 0)
    def _():
        pl.semaphore_signal(barrier, inc=1, device_id=(y, f - 1), device_id_type=MESH)

    @pl.when(f < FP - 1)
    def _():
        pl.semaphore_signal(barrier, inc=1, device_id=(y, f + 1), device_id_type=MESH)

    @pl.when(f == 0)
    def _():
        up_ref[...] = jnp.zeros_like(up_ref)

    @pl.when(f == FP - 1)
    def _():
        down_ref[...] = jnp.zeros_like(down_ref)

    taps_ref[...] = jnp.zeros_like(taps_ref)
    taps_ref[0:2, 4 : 4 + bank_ref.shape[2]] = bank_ref[id_ref[0, 0]].astype(jnp.float32)

    inner = (f > 0) & (f < FP - 1)

    @pl.when(inner)
    def _():
        pl.semaphore_wait(barrier, 2)

    @pl.when(jnp.logical_not(inner))
    def _():
        pl.semaphore_wait(barrier, 1)

    @pl.when(f < FP - 1)
    def _():
        to_next.start()

    @pl.when(f > 0)
    def _():
        to_last.start()

    route(inv_ref, gap_ref, tile_ref, off_ref, src_ref, meta_ref)

    @pl.when(f < FP - 1)
    def _():
        to_next.wait_send()
        to_last.wait_recv()

    @pl.when(f > 0)
    def _():
        to_last.wait_send()
        to_next.wait_recv()


def route(inv_ref, gap_ref, tile_ref, off_ref, src_ref, meta_ref):
    segs, _, rows = tile_ref.shape
    inv = inv_ref[0, 0]
    gap = gap_ref[0, 0]
    before = lax.broadcasted_iota(jnp.int32, (rows, rows), 0)
    after = lax.broadcasted_iota(jnp.int32, (rows, rows), 1)
    upper = (before < after).astype(jnp.float32).astype(jnp.bfloat16)
    tile_iota = lax.broadcasted_iota(jnp.int32, (DEVICES, rows), 0)
    slot_iota = lax.broadcasted_iota(jnp.int32, (CAP, rows), 0)
    row = lax.broadcasted_iota(jnp.int32, (1, rows), 1)
    open_row = jnp.where((row >= gap) & (row < gap + GAP), 0.0, 1.0)
    row_f = row.astype(jnp.float32)
    base = jnp.zeros((DEVICES, 1), jnp.float32)
    found = jnp.zeros((DEVICES, 5 * CAP), jnp.float32)
    for s in range(segs):
        hot = (tile_iota == tile_ref[s]).astype(jnp.float32)
        hot_b = hot.astype(jnp.bfloat16)
        inside = jnp.dot(hot_b, upper, preferred_element_type=jnp.float32)
        rank = jnp.sum(hot * (inside + base), axis=0, keepdims=True)
        base = base + jnp.sum(hot, axis=1, keepdims=True)
        at_slot = (slot_iota == rank.astype(jnp.int32)).astype(jnp.float32)
        offset = off_ref[s : s + 1, :] + 1
        packed = jnp.concatenate(
            [
                at_slot * float(s),
                at_slot * row_f,
                at_slot * (offset >> 6).astype(jnp.float32),
                at_slot * (offset & 63).astype(jnp.float32),
                at_slot * open_row,
            ],
            axis=0,
        ).astype(jnp.bfloat16)
        found = found + lax.dot_general(hot_b, packed, NT, preferred_element_type=jnp.float32)
    source = found[:, :CAP] * float(rows) + found[:, CAP : 2 * CAP]
    src_ref[...] = source.astype(jnp.int32)
    offset = found[:, 2 * CAP : 3 * CAP] * 64.0 + found[:, 3 * CAP : 4 * CAP] - 1.0
    meta_ref[:, 0, :] = jnp.concatenate([offset, found[:, 4 * CAP :] * inv], axis=1)


def band(taps, rows, width, shift):
    wide = jnp.broadcast_to(taps[:, :width], (rows, width))
    return pltpu.roll(wide, shift - 4, 1, stride=1, stride_axis=0).astype(jnp.bfloat16)


PARTS = 8
SPAN = 512
GROUP = 8


def fused_kernel(
    inv_ref, gap_ref, src_ref, taps_ref, up_ref, raw_ref, down_ref, meta_ref, total,
    framed, vertical, pieces, stage, sent, got, gmeta, vsend, vrecv, msend, mrecv, local,
):
    barrier = pltpu.get_barrier_semaphore()
    groups = DEVICES // GROUP

    def greet(j, carry):
        at = corner(j)
        for i in range(GROUP):
            if i:
                pl.semaphore_signal(barrier, inc=1, device_id=target(at, i), device_id_type=MESH)
            else:

                @pl.when(j > 0)
                def _():
                    pl.semaphore_signal(
                        barrier, inc=1, device_id=target(at, 0), device_id_type=MESH
                    )

        return carry

    lax.fori_loop(0, groups, greet, 0)
    rows, cols = raw_ref.shape
    half = SEG
    vtap = taps_ref[0:1, :]
    htap = taps_ref[1:2, :]
    framed[0:32, :] = jnp.zeros((32, cols), jnp.bfloat16)
    framed[32:64, :] = up_ref[...]
    framed[64 : 64 + rows, :] = raw_ref[...]
    framed[64 + rows : 96 + rows, :] = down_ref[...]
    framed[96 + rows : 128 + rows, :] = jnp.zeros((32, cols), jnp.bfloat16)
    vertical[:, :SEG] = jnp.zeros((rows, SEG), jnp.bfloat16)
    vertical[:, SEG + cols :] = jnp.zeros((rows, SEG), jnp.bfloat16)
    vband = band(vtap, half, 256, 44)
    hband = band(htap, 256, 512, 108)
    for n in range(cols // 512):
        for m in range(rows // half):
            made = jnp.dot(
                vband,
                framed[m * half : m * half + 256, n * 512 : (n + 1) * 512],
                preferred_element_type=jnp.float32,
            )
            vertical[m * half : (m + 1) * half, SEG + n * 512 : SEG + (n + 1) * 512] = made.astype(
                jnp.bfloat16
            )
    row = lax.broadcasted_iota(jnp.int32, (rows, 256), 0)
    gap = gap_ref[0, 0]
    weight = jnp.where((row >= gap) & (row < gap + GAP), 0.0, inv_ref[0, 0])
    for n in range(cols // 256):
        made = lax.dot_general(
            vertical[:, n * 256 : n * 256 + 512], hband, NT, preferred_element_type=jnp.float32
        )
        made = made.astype(jnp.bfloat16).astype(jnp.float32) * weight
        pieces[2 * n * rows : (2 * n + 1) * rows, :] = made[:, :SEG]
        pieces[(2 * n + 1) * rows : (2 * n + 2) * rows, :] = made[:, SEG:]

    def copies(j, i, at):
        step = j * GROUP + i
        ty, tf = target(at, i)
        return (
            pltpu.make_async_remote_copy(
                src_ref=meta_ref.at[ty * FP + tf], dst_ref=gmeta.at[step],
                send_sem=msend.at[step], recv_sem=mrecv.at[step],
                device_id=(ty, tf), device_id_type=MESH,
            ),
            pltpu.make_async_remote_copy(
                src_ref=sent.at[step], dst_ref=got.at[step],
                send_sem=vsend.at[step], recv_sem=vrecv.at[step],
                device_id=(ty, tf), device_id_type=MESH,
            ),
        )

    me = lax.axis_index("expo") * FP + lax.axis_index("fp")
    own_meta = pltpu.make_async_copy(meta_ref.at[me], gmeta.at[0], local.at[0])
    own = pltpu.make_async_copy(sent.at[0], got.at[0], local.at[1])
    pl.semaphore_wait(barrier, DEVICES - 1)

    def pack(j, carry):
        at = corner(j)
        for i in range(GROUP):
            ty, tf = target(at, i)
            to = ty * FP + tf
            for k in range(CAP):
                stage[i, k : k + 1, :] = pieces[pl.ds(src_ref[to, k], 1), :]
            sent[j * GROUP + i] = stage[i].astype(jnp.bfloat16)
            if i:
                for copy in copies(j, i, at):
                    copy.start()
            else:

                @pl.when(j > 0)
                def _():
                    for copy in copies(j, 0, at):
                        copy.start()

                @pl.when(j == 0)
                def _():
                    own_meta.start()
                    own.start()

        return carry

    lax.fori_loop(0, groups, pack, 0)
    span_iota = lax.broadcasted_iota(jnp.int32, (SPAN, GROUP * CAP), 0)
    lane = lax.broadcasted_iota(jnp.int32, (GROUP * CAP, SEG), 1)
    total[...] = jnp.zeros_like(total)

    def chunk(j, carry):
        at = corner(j)
        for i in range(GROUP):
            if i:
                for copy in copies(j, i, at):
                    copy.wait_recv()
            else:

                @pl.when(j > 0)
                def _():
                    for copy in copies(j, 0, at):
                        copy.wait_recv()

                @pl.when(j == 0)
                def _():
                    own_meta.wait()
                    own.wait()

        meta = gmeta[pl.ds(j * GROUP, GROUP), 0, :]
        slots = jnp.concatenate([meta[i : i + 1, :CAP] for i in range(GROUP)], axis=1)
        slots = slots.astype(jnp.int32) & (SPAN - 1)
        hot = (span_iota == slots).astype(jnp.float32).astype(jnp.bfloat16)
        turned = meta.T
        column = jnp.concatenate([turned[:CAP, i : i + 1] for i in range(GROUP)], axis=0)
        part = jnp.broadcast_to(column, (GROUP * CAP, SEG)).astype(jnp.int32) >> 9
        weight = jnp.concatenate([turned[CAP:, i : i + 1] for i in range(GROUP)], axis=0)
        weight = jnp.broadcast_to(weight, (GROUP * CAP, SEG))
        high = weight.astype(jnp.bfloat16).astype(jnp.float32)
        spread = jnp.where(lane == part, high, 0.0)
        spread = spread + jnp.where(lane == part + PARTS, jnp.where(part < 0, 0.0, weight - high), 0.0)
        values = got[pl.ds(j * GROUP, GROUP)].reshape(GROUP * CAP, SEG)
        values = values.astype(jnp.float32)
        masked = [jnp.where(part == a, values, 0.0).astype(jnp.bfloat16) for a in range(PARTS)]
        right = jnp.concatenate(masked + [spread.astype(jnp.bfloat16)], axis=1)
        total[...] += jnp.dot(hot, right, preferred_element_type=jnp.float32)
        return carry

    lax.fori_loop(0, groups, chunk, 0)

    def finish(j, carry):
        at = corner(j)
        for i in range(GROUP):
            if i:
                for copy in copies(j, i, at):
                    copy.wait_send()
            else:

                @pl.when(j > 0)
                def _():
                    for copy in copies(j, 0, at):
                        copy.wait_send()

        return carry

    lax.fori_loop(0, groups, finish, 0)


def mean_kernel(total_ref, image_ref, weight_ref, mean, sems):
    sums = total_ref[:, PARTS * SEG :]
    sums = sums[:, :PARTS] + sums[:, PARTS : 2 * PARTS]
    scale = 1.0 / jnp.maximum(sums, 1.0)
    copies = []
    for a in range(PARTS):
        slots = slice(a * SPAN, (a + 1) * SPAN)
        mean[slots, :] = total_ref[:, a * SEG : (a + 1) * SEG] * scale[:, a : a + 1]
        copies.append(
            pltpu.make_async_copy(
                mean.at[pl.ds(a * SPAN, SPAN)], image_ref.at[pl.ds(a * SPAN, SPAN)], sems.at[a]
            )
        )
        copies[-1].start()
    turned = sums.T
    for a in range(PARTS):
        weight_ref[:, a * SPAN : (a + 1) * SPAN] = turned[a : a + 1, :]
    for copy in copies:
        copy.wait()


def body(raw_pixels, kernel_bank, kernel_ids, inv_var, gap_start, warp_tile, warp_offset):
    raw = raw_pixels[0]
    rows, cols = raw.shape
    tiles = jnp.transpose(warp_tile[0], (1, 2, 0))
    offsets = warp_offset[0].T
    smem = pl.BlockSpec(memory_space=pltpu.SMEM)
    vmem = pl.BlockSpec(memory_space=pltpu.VMEM)
    hbm = pl.BlockSpec(memory_space=pl.ANY)
    dma = pltpu.SemaphoreType.DMA
    source, meta, taps, above, below = pl.pallas_call(
        front_kernel,
        out_shape=(
            jax.ShapeDtypeStruct((DEVICES, CAP), jnp.int32),
            jax.ShapeDtypeStruct((DEVICES, 1, 2 * CAP), jnp.float32),
            jax.ShapeDtypeStruct((8, 512), jnp.float32),
            jax.ShapeDtypeStruct((HALO, cols), jnp.bfloat16),
            jax.ShapeDtypeStruct((HALO, cols), jnp.bfloat16),
        ),
        in_specs=[smem, smem, smem, vmem, vmem, vmem, hbm],
        out_specs=(vmem,) * 5,
        scratch_shapes=[dma((2,)), dma((2,))],
        compiler_params=pltpu.CompilerParams(
            collective_id=0, has_side_effects=True, vmem_limit_bytes=16 << 20
        ),
        name="front",
    )(kernel_ids, inv_var, gap_start, kernel_bank, tiles, offsets, raw)
    total = pl.pallas_call(
        fused_kernel,
        out_shape=jax.ShapeDtypeStruct((SPAN, (PARTS + 1) * SEG), jnp.float32),
        in_specs=[smem, smem, smem] + [vmem] * 5,
        out_specs=vmem,
        scratch_shapes=[
            pltpu.VMEM((rows + 128, cols), jnp.bfloat16),
            pltpu.VMEM((rows, cols + 2 * SEG), jnp.bfloat16),
            pltpu.VMEM((rows * cols // SEG, SEG), jnp.float32),
            pltpu.VMEM((GROUP, CAP, SEG), jnp.float32),
            pltpu.VMEM((DEVICES, CAP, SEG), jnp.bfloat16),
            pltpu.VMEM((DEVICES, CAP, SEG), jnp.bfloat16),
            pltpu.VMEM((DEVICES, 1, 2 * CAP), jnp.float32),
            dma((DEVICES,)), dma((DEVICES,)), dma((DEVICES,)), dma((DEVICES,)), dma((2,)),
        ],
        compiler_params=pltpu.CompilerParams(
            collective_id=1, has_side_effects=True, vmem_limit_bytes=40 << 20
        ),
        name="fused",
    )(inv_var, gap_start, source, taps, above, raw, below, meta)
    image, weight = pl.pallas_call(
        mean_kernel,
        out_shape=(
            jax.ShapeDtypeStruct((PARTS * SPAN, SEG), jnp.float32),
            jax.ShapeDtypeStruct((1, PARTS * SPAN), jnp.float32),
        ),
        in_specs=[vmem],
        out_specs=(hbm, vmem),
        scratch_shapes=[pltpu.VMEM((PARTS * SPAN, SEG), jnp.float32), dma((PARTS,))],
        compiler_params=pltpu.CompilerParams(vmem_limit_bytes=16 << 20),
        name="mean",
    )(total)
    return image[None], weight


def solution(mesh):
    in_specs = (
        P("expo", "fp", None),
        P(),
        P("expo", "fp"),
        P("expo", "fp"),
        P("expo", "fp"),
        P("expo", "fp", None, None),
        P("expo", "fp", None),
    )
    out_specs = (P(("expo", "fp"), None, None), P(("expo", "fp"), None))
    return jax.shard_map(body, mesh=mesh, in_specs=in_specs, out_specs=out_specs, check_vma=False)
```

time: 99.9 us -> 70.3 us (0.70)
  the two profiles are of different devices: /device:TPU:1 before, /device:TPU:35 now
where the time goes in v2:
time: 70.3 us; the launch traced here: 70 us
  Pallas kernels  62.8 us (89%)
  local copies, waits for them, and re-layouts  4.56 us (6%)
  between operations  2.6 us (4%)
    pallas_call x1, Pallas kernels, body(): pl.pallas_call(fused_kernel, out_shape=jax.ShapeDtypeStruct((SPAN, (PARTS...  54.7 us
    pallas_call x1, Pallas kernels, body(): pl.pallas_call(front_kernel, out_shape=(jax.ShapeDtypeStruct((DEVICES, CA...  5.96 us
    unnamed x10, local copies, waits for them, and re-layouts  4.56 us
    pallas_call x1, Pallas kernels, body(): pl.pallas_call(mean_kernel, out_shape=(jax.ShapeDtypeStruct((PARTS * SPAN...  2.19 us

profile of v2, /device:TPU:35, one launch (start us, length us, event | category | flops | bytes accessed | tf_op | source)
XLA Modules:
  0.0 70.0 jit_solution(15058592655322476873)
XLA Ops:
  2.6 0.0 copy-start
  2.6 1.2 %copy-done = bf16[1,256,2048]{2,1,0:T(8,128)(2,1)S(1)} copy-done((bf16[1,256,2048]{2,1,0:T(8,128)(2,1)S(1)}, bf16[1,256,2048]{2,1,0:T(8,128)(2,1)}, u32[]{:S(2)}) %copy-start) | copy-done | bytes 1048600
  3.8 0.0 copy-start.2
  3.8 0.7 %copy-done.2 = s32[1,256,16,1]{1,3,2,0:T(1,128)S(1)} copy-done((s32[1,256,16,1]{1,3,2,0:T(1,128)S(1)}, s32[1,256,16,1]{1,3,2,0:T(1,128)}, u32[]{:S(2)}) %copy-start.2) | copy-done | bytes 16408
  4.5 0.0 copy-start.3
  4.5 0.7 %copy-done.3 = s32[1,256,16]{1,2,0:T(8,128)S(1)} copy-done((s32[1,256,16]{1,2,0:T(8,128)S(1)}, s32[1,256,16]{1,2,0:T(8,128)}, u32[]{:S(2)}) %copy-start.3) | copy-done | bytes 16408
  5.2 0.0 copy-start.4
  5.2 0.7 copy-done.4
  5.9 6.0 %front.1 = (s32[128,64]{1,0:T(8,128)S(1)}, f32[128,1,128]{2,1,0:T(1,128)S(1)}, f32[8,512]{1,0:T(8,128)S(1)}, bf16[32,2048]{1,0:T(8,128)(2,1)S(1)}, bf16[32,2048]{1,0:T(8,128)(2,1)S(1)}) custom-call(s32[1,1]{1,0:T(1,128)S(6)} %copy.9.id_ref, f32[1,1]{1,0:T(1,128)S(6)} %copy.10.inv_ref, s32[1,1]{1,0:T(1,128)S(6)} %copy.11.gap_ref, ...), custom_call_target="tpu_custom_call" | custom-call | tf_op jit(solution)/shard_map/front/pallas_call | solution.py:346
  11.9 0.0 copy-start.1
  11.9 1.2 %copy-done.1 = bf16[1,256,2048]{2,1,0:T(8,128)(2,1)S(1)} copy-done((bf16[1,256,2048]{2,1,0:T(8,128)(2,1)S(1)}, bf16[1,256,2048]{2,1,0:T(8,128)(2,1)}, u32[]{:S(2)}) %copy-start.1) | copy-done | bytes 1048600
  13.1 54.7 %fused.1.total_ref = f32[512,1152]{1,0:T(8,128)S(1)} custom-call(f32[1,1]{1,0:T(1,128)S(6)} %copy.10.inv_ref, s32[1,1]{1,0:T(1,128)S(6)} %copy.11.gap_ref, s32[128,64]{1,0:T(8,128)S(1)} %get-tuple-element.9.src_ref, f32[8,512]{1,0:T(8,128)S(1)} %get-tuple-element.10.taps_ref, bf16[32,2048]{1,0:T(8,128)(2,1)S(1)} %get-tuple-element.11.up_ref, ...), custom_call_target="tpu_custom_call" | custom-call | tf_op jit(solution)/shard_map/fused/pallas_call | solution.py:363
  67.8 2.2 %mean.1 = (f32[4096,128]{1,0:T(8,128)}, f32[1,4096]{1,0:T(1,128)}) custom-call(f32[512,1152]{1,0:T(8,128)S(1)} %fused.1.total_ref), custom_call_target="tpu_custom_call" | custom-call | tf_op jit(solution)/shard_map/mean/pallas_call | solution.py:383
Async XLA Ops:
  2.6 1.2 %copy-start = (bf16[1,256,2048]{2,1,0:T(8,128)(2,1)S(1)}, bf16[1,256,2048]{2,1,0:T(8,128)(2,1)}, u32[]{:S(2)}) copy-start(bf16[1,256,2048]{2,1,0:T(8,128)(2,1)} %param.7) | copy-start | bytes 3145732
  3.8 0.7 %copy-start.2 = (s32[1,256,16,1]{1,3,2,0:T(1,128)S(1)}, s32[1,256,16,1]{1,3,2,0:T(1,128)}, u32[]{:S(2)}) copy-start(s32[1,256,16,1]{1,3,2,0:T(1,128)} %param.12) | copy-start | bytes 49156
  4.5 0.7 %copy-start.3 = (s32[1,256,16]{1,2,0:T(8,128)S(1)}, s32[1,256,16]{1,2,0:T(8,128)}, u32[]{:S(2)}) copy-start(s32[1,256,16]{1,2,0:T(8,128)} %param.13) | copy-start | bytes 49156
  5.2 0.7 copy-start.4
  11.9 1.2 %copy-start.1 = (bf16[1,256,2048]{2,1,0:T(8,128)(2,1)S(1)}, bf16[1,256,2048]{2,1,0:T(8,128)(2,1)}, u32[]{:S(2)}) copy-start(bf16[1,256,2048]{2,1,0:T(8,128)(2,1)} %param.7) | copy-start | bytes 3145732

commit v3 on v2

--- a/solution.py
+++ b/solution.py
@@ -31,12 +31,21 @@
 
 
 def front_kernel(
-    id_ref, inv_ref, gap_ref, bank_ref, tile_ref, off_ref, raw_ref,
+    id_ref, inv_ref, gap_ref, bank_hbm, tile_hbm, off_hbm, raw_ref,
     src_ref, meta_ref, taps_ref, up_ref, down_ref, send_sem, recv_sem,
+    bank_ref, tile_ref, off_ref, load_sem,
 ):
     y = lax.axis_index("expo")
     f = lax.axis_index("fp")
     top = raw_ref.shape[0] - HALO
+    loads = [
+        pltpu.make_async_copy(source, ref, load_sem.at[n])
+        for n, (source, ref) in enumerate(
+            [(bank_hbm, bank_ref), (tile_hbm, tile_ref), (off_hbm, off_ref)]
+        )
+    ]
+    for load in loads:
+        load.start()
     barrier = pltpu.get_barrier_semaphore()
     to_next = pltpu.make_async_remote_copy(
         src_ref=raw_ref.at[pl.ds(top, HALO)], dst_ref=up_ref,
@@ -65,6 +74,8 @@
     def _():
         down_ref[...] = jnp.zeros_like(down_ref)
 
+    for load in loads:
+        load.wait()
     taps_ref[...] = jnp.zeros_like(taps_ref)
     taps_ref[0:2, 4 : 4 + bank_ref.shape[2]] = bank_ref[id_ref[0, 0]].astype(jnp.float32)
 
@@ -149,41 +160,41 @@
 
 
 def fused_kernel(
-    inv_ref, gap_ref, src_ref, taps_ref, up_ref, raw_ref, down_ref, meta_ref, total,
+    inv_ref, gap_ref, src_ref, taps_ref, up_ref, raw_ref, down_ref, meta_ref, total, weights,
     framed, vertical, pieces, stage, sent, got, gmeta, vsend, vrecv, msend, mrecv, local,
 ):
     barrier = pltpu.get_barrier_semaphore()
     groups = DEVICES // GROUP
 
-    def greet(j, carry):
-        at = corner(j)
-        for i in range(GROUP):
-            if i:
-                pl.semaphore_signal(barrier, inc=1, device_id=target(at, i), device_id_type=MESH)
-            else:
-
-                @pl.when(j > 0)
-                def _():
-                    pl.semaphore_signal(
-                        barrier, inc=1, device_id=target(at, 0), device_id_type=MESH
-                    )
-
-        return carry
-
-    lax.fori_loop(0, groups, greet, 0)
+    y = lax.axis_index("expo")
+    f = lax.axis_index("fp")
+    ys = [lax.rem(y + k, 4) for k in range(4)]
+    xs = [lax.rem(f // 8 + k, 4) * 8 for k in range(4)]
+    zs = [lax.rem(f // 2 + k, 4) * 2 for k in range(4)]
+    cores = [lax.rem(f + k, 2) for k in range(2)]
+    for step in range(1, DEVICES):
+        a, b, c = step // 2 % 4, step // 8 % 4, step // 32
+        to = (ys[(a + c) % 4], xs[(a + b) % 4] + zs[(a + b + c) % 4] + cores[step % 2])
+        pl.semaphore_signal(barrier, inc=1, device_id=to, device_id_type=MESH)
     rows, cols = raw_ref.shape
     half = SEG
     vtap = taps_ref[0:1, :]
     htap = taps_ref[1:2, :]
     framed[0:32, :] = jnp.zeros((32, cols), jnp.bfloat16)
-    framed[32:64, :] = up_ref[...]
-    framed[64 : 64 + rows, :] = raw_ref[...]
-    framed[64 + rows : 96 + rows, :] = down_ref[...]
+    loads = [
+        pltpu.make_async_copy(raw_ref, framed.at[pl.ds(64, rows)], local.at[2]),
+        pltpu.make_async_copy(up_ref, framed.at[pl.ds(32, HALO)], local.at[3]),
+        pltpu.make_async_copy(down_ref, framed.at[pl.ds(64 + rows, HALO)], local.at[4]),
+    ]
+    for load in loads:
+        load.start()
     framed[96 + rows : 128 + rows, :] = jnp.zeros((32, cols), jnp.bfloat16)
     vertical[:, :SEG] = jnp.zeros((rows, SEG), jnp.bfloat16)
     vertical[:, SEG + cols :] = jnp.zeros((rows, SEG), jnp.bfloat16)
     vband = band(vtap, half, 256, 44)
     hband = band(htap, 256, 512, 108)
+    for load in loads:
+        load.wait()
     for n in range(cols // 512):
         for m in range(rows // half):
             made = jnp.dot(
@@ -211,12 +222,12 @@
         return (
             pltpu.make_async_remote_copy(
                 src_ref=meta_ref.at[ty * FP + tf], dst_ref=gmeta.at[step],
-                send_sem=msend.at[step], recv_sem=mrecv.at[step],
+                send_sem=msend, recv_sem=mrecv.at[j],
                 device_id=(ty, tf), device_id_type=MESH,
             ),
             pltpu.make_async_remote_copy(
                 src_ref=sent.at[step], dst_ref=got.at[step],
-                send_sem=vsend.at[step], recv_sem=vrecv.at[step],
+                send_sem=vsend, recv_sem=vrecv.at[j],
                 device_id=(ty, tf), device_id_type=MESH,
             ),
         )
@@ -252,71 +263,61 @@
         return carry
 
     lax.fori_loop(0, groups, pack, 0)
-    span_iota = lax.broadcasted_iota(jnp.int32, (SPAN, GROUP * CAP), 0)
-    lane = lax.broadcasted_iota(jnp.int32, (GROUP * CAP, SEG), 1)
+    span_iota = lax.broadcasted_iota(jnp.int32, (SPAN, GROUP * CAP), 0).astype(jnp.int16)
+    part_iota = lax.broadcasted_iota(jnp.int32, (2 * PARTS, GROUP * CAP), 0)
     total[...] = jnp.zeros_like(total)
+    weights[...] = jnp.zeros_like(weights)
+
+    def arrived(j, first, count):
+        for buffer, sem in ((gmeta, mrecv), (got, vrecv)):
+            slots = buffer.at[pl.ds(j * GROUP + first, count)]
+            pltpu.make_async_copy(slots, slots, sem.at[j]).wait()
 
     def chunk(j, carry):
-        at = corner(j)
-        for i in range(GROUP):
-            if i:
-                for copy in copies(j, i, at):
-                    copy.wait_recv()
-            else:
-
-                @pl.when(j > 0)
-                def _():
-                    for copy in copies(j, 0, at):
-                        copy.wait_recv()
-
-                @pl.when(j == 0)
-                def _():
-                    own_meta.wait()
-                    own.wait()
+        @pl.when(j > 0)
+        def _():
+            arrived(j, 0, GROUP)
+
+        @pl.when(j == 0)
+        def _():
+            own_meta.wait()
+            own.wait()
+            arrived(0, 1, GROUP - 1)
 
         meta = gmeta[pl.ds(j * GROUP, GROUP), 0, :]
         slots = jnp.concatenate([meta[i : i + 1, :CAP] for i in range(GROUP)], axis=1)
-        slots = slots.astype(jnp.int32) & (SPAN - 1)
-        hot = (span_iota == slots).astype(jnp.float32).astype(jnp.bfloat16)
-        turned = meta.T
+        weight = jnp.concatenate([meta[i : i + 1, CAP:] for i in range(GROUP)], axis=1)
+        slots = slots.astype(jnp.int32)
+        inside = jnp.broadcast_to(slots & (SPAN - 1), (16, GROUP * CAP)).astype(jnp.int16)
+        inside = jnp.broadcast_to(inside[:1], (SPAN, GROUP * CAP))
+        hot = jnp.where(span_iota == inside, jnp.bfloat16(1), jnp.bfloat16(0))
+        high = weight.astype(jnp.bfloat16).astype(jnp.float32)
+        part = slots >> 9
+        spread = jnp.where(part_iota == part, high, 0.0)
+        spread = jnp.where((part_iota == part + PARTS) & (part >= 0), weight - high, spread)
+        weights[...] += lax.dot_general(
+            spread.astype(jnp.bfloat16), hot, NT, preferred_element_type=jnp.float32
+        )
+        turned = jnp.floor(meta * (1.0 / SPAN)).T
         column = jnp.concatenate([turned[:CAP, i : i + 1] for i in range(GROUP)], axis=0)
-        part = jnp.broadcast_to(column, (GROUP * CAP, SEG)).astype(jnp.int32) >> 9
-        weight = jnp.concatenate([turned[CAP:, i : i + 1] for i in range(GROUP)], axis=0)
-        weight = jnp.broadcast_to(weight, (GROUP * CAP, SEG))
-        high = weight.astype(jnp.bfloat16).astype(jnp.float32)
-        spread = jnp.where(lane == part, high, 0.0)
-        spread = spread + jnp.where(lane == part + PARTS, jnp.where(part < 0, 0.0, weight - high), 0.0)
+        part = jnp.broadcast_to(column, (GROUP * CAP, SEG)).astype(jnp.bfloat16)
         values = got[pl.ds(j * GROUP, GROUP)].reshape(GROUP * CAP, SEG)
-        values = values.astype(jnp.float32)
-        masked = [jnp.where(part == a, values, 0.0).astype(jnp.bfloat16) for a in range(PARTS)]
-        right = jnp.concatenate(masked + [spread.astype(jnp.bfloat16)], axis=1)
+        none = jnp.zeros_like(values)
+        masked = [jnp.where(part == jnp.bfloat16(a), values, none) for a in range(PARTS)]
+        right = jnp.concatenate(masked, axis=1)
         total[...] += jnp.dot(hot, right, preferred_element_type=jnp.float32)
         return carry
 
     lax.fori_loop(0, groups, chunk, 0)
 
-    def finish(j, carry):
-        at = corner(j)
-        for i in range(GROUP):
-            if i:
-                for copy in copies(j, i, at):
-                    copy.wait_send()
-            else:
-
-                @pl.when(j > 0)
-                def _():
-                    for copy in copies(j, 0, at):
-                        copy.wait_send()
-
-        return carry
-
-    lax.fori_loop(0, groups, finish, 0)
-
-
-def mean_kernel(total_ref, image_ref, weight_ref, mean, sems):
-    sums = total_ref[:, PARTS * SEG :]
-    sums = sums[:, :PARTS] + sums[:, PARTS : 2 * PARTS]
-    scale = 1.0 / jnp.maximum(sums, 1.0)
+    for buffer, sem in ((meta_ref, msend), (sent, vsend)):
+        slots = buffer.at[pl.ds(1, DEVICES - 1)]
+        pltpu.make_async_copy(slots, slots, sem).wait()
+
+
+def mean_kernel(total_ref, sums_ref, image_ref, weight_ref, mean, sems):
+    sums = sums_ref[:PARTS, :] + sums_ref[PARTS:, :]
+    scale = (1.0 / jnp.maximum(sums, 1.0)).T
     copies = []
     for a in range(PARTS):
         slots = slice(a * SPAN, (a + 1) * SPAN)
@@ -327,9 +328,8 @@
             )
         )
         copies[-1].start()
-    turned = sums.T
     for a in range(PARTS):
-        weight_ref[:, a * SPAN : (a + 1) * SPAN] = turned[a : a + 1, :]
+        weight_ref[:, a * SPAN : (a + 1) * SPAN] = sums[a : a + 1, :]
     for copy in copies:
         copy.wait()
 
@@ -342,6 +342,7 @@
     smem = pl.BlockSpec(memory_space=pltpu.SMEM)
     vmem = pl.BlockSpec(memory_space=pltpu.VMEM)
     hbm = pl.BlockSpec(memory_space=pl.ANY)
+    fixed = pl.BlockSpec(memory_space=pltpu.HBM)
     dma = pltpu.SemaphoreType.DMA
     source, meta, taps, above, below = pl.pallas_call(
         front_kernel,
@@ -352,19 +353,28 @@
             jax.ShapeDtypeStruct((HALO, cols), jnp.bfloat16),
             jax.ShapeDtypeStruct((HALO, cols), jnp.bfloat16),
         ),
-        in_specs=[smem, smem, smem, vmem, vmem, vmem, hbm],
+        in_specs=[smem, smem, smem, fixed, fixed, fixed, fixed],
         out_specs=(vmem,) * 5,
-        scratch_shapes=[dma((2,)), dma((2,))],
+        scratch_shapes=[
+            dma((2,)), dma((2,)),
+            pltpu.VMEM(kernel_bank.shape, kernel_bank.dtype),
+            pltpu.VMEM(tiles.shape, tiles.dtype),
+            pltpu.VMEM(offsets.shape, offsets.dtype),
+            dma((3,)),
+        ],
         compiler_params=pltpu.CompilerParams(
             collective_id=0, has_side_effects=True, vmem_limit_bytes=16 << 20
         ),
         name="front",
     )(kernel_ids, inv_var, gap_start, kernel_bank, tiles, offsets, raw)
-    total = pl.pallas_call(
+    total, sums = pl.pallas_call(
         fused_kernel,
-        out_shape=jax.ShapeDtypeStruct((SPAN, (PARTS + 1) * SEG), jnp.float32),
-        in_specs=[smem, smem, smem] + [vmem] * 5,
-        out_specs=vmem,
+        out_shape=(
+            jax.ShapeDtypeStruct((SPAN, PARTS * SEG), jnp.float32),
+            jax.ShapeDtypeStruct((2 * PARTS, SPAN), jnp.float32),
+        ),
+        in_specs=[smem, smem, smem, vmem, hbm, fixed, hbm, vmem],
+        out_specs=(vmem, vmem),
         scratch_shapes=[
             pltpu.VMEM((rows + 128, cols), jnp.bfloat16),
             pltpu.VMEM((rows, cols + 2 * SEG), jnp.bfloat16),
@@ -373,7 +383,7 @@
             pltpu.VMEM((DEVICES, CAP, SEG), jnp.bfloat16),
             pltpu.VMEM((DEVICES, CAP, SEG), jnp.bfloat16),
             pltpu.VMEM((DEVICES, 1, 2 * CAP), jnp.float32),
-            dma((DEVICES,)), dma((DEVICES,)), dma((DEVICES,)), dma((DEVICES,)), dma((2,)),
+            dma, dma((DEVICES // GROUP,)), dma, dma((DEVICES // GROUP,)), dma((5,)),
         ],
         compiler_params=pltpu.CompilerParams(
             collective_id=1, has_side_effects=True, vmem_limit_bytes=40 << 20
@@ -386,12 +396,12 @@
             jax.ShapeDtypeStruct((PARTS * SPAN, SEG), jnp.float32),
             jax.ShapeDtypeStruct((1, PARTS * SPAN), jnp.float32),
         ),
-        in_specs=[vmem],
-        out_specs=(hbm, vmem),
+        in_specs=[vmem, vmem],
+        out_specs=(fixed, vmem),
         scratch_shapes=[pltpu.VMEM((PARTS * SPAN, SEG), jnp.float32), dma((PARTS,))],
         compiler_params=pltpu.CompilerParams(vmem_limit_bytes=16 << 20),
         name="mean",
-    )(total)
+    )(total, sums)
     return image[None], weight
 
 

time: 70.3 us -> 62.5 us (0.89)
  Pallas kernels: 62.8 us -> 55 us
    pallas_call x1, Pallas kernels: 54.7 us -> 46.7 us  [body(): pl.pallas_call(fused_kernel, out_shape=(jax.ShapeDtypeStruct((SPAN, PARTS...]
where the time goes in v3:
time: 62.5 us; the launch traced here: 62.1 us
  Pallas kernels  55 us (88%)
  local copies, waits for them, and re-layouts  4.56 us (7%)
  between operations  2.6 us (4%)
    pallas_call x1, Pallas kernels, body(): pl.pallas_call(fused_kernel, out_shape=(jax.ShapeDtypeStruct((SPAN, PARTS...  46.7 us
    pallas_call x1, Pallas kernels, body(): pl.pallas_call(front_kernel, out_shape=(jax.ShapeDtypeStruct((DEVICES, CA...  6.04 us
    unnamed x10, local copies, waits for them, and re-layouts  4.56 us
    pallas_call x1, Pallas kernels, body(): pl.pallas_call(mean_kernel, out_shape=(jax.ShapeDtypeStruct((PARTS * SPAN...  2.24 us

profile of v3, /device:TPU:35, one launch (start us, length us, event | category | flops | bytes accessed | tf_op | source)
XLA Modules:
  0.0 62.1 jit_solution(11234145076789197536)
XLA Ops:
  2.6 0.0 copy-start
  2.6 1.2 %copy-done = bf16[1,256,2048]{2,1,0:T(8,128)(2,1)S(1)} copy-done((bf16[1,256,2048]{2,1,0:T(8,128)(2,1)S(1)}, bf16[1,256,2048]{2,1,0:T(8,128)(2,1)}, u32[]{:S(2)}) %copy-start) | copy-done | bytes 1048600
  3.8 0.0 copy-start.2
  3.8 0.7 %copy-done.2 = s32[1,256,16,1]{1,3,2,0:T(1,128)S(1)} copy-done((s32[1,256,16,1]{1,3,2,0:T(1,128)S(1)}, s32[1,256,16,1]{1,3,2,0:T(1,128)}, u32[]{:S(2)}) %copy-start.2) | copy-done | bytes 16408
  4.5 0.0 copy-start.3
  4.5 0.7 %copy-done.3 = s32[1,256,16]{1,2,0:T(8,128)S(1)} copy-done((s32[1,256,16]{1,2,0:T(8,128)S(1)}, s32[1,256,16]{1,2,0:T(8,128)}, u32[]{:S(2)}) %copy-start.3) | copy-done | bytes 16408
  5.2 0.0 copy-start.4
  5.2 0.7 %copy-done.4 = bf16[8,2,41]{2,1,0:T(2,128)(2,1)S(1)} copy-done((bf16[8,2,41]{2,1,0:T(2,128)(2,1)S(1)}, bf16[8,2,41]{2,1,0:T(2,128)(2,1)}, u32[]{:S(2)}) %copy-start.4) | copy-done | bytes 1336
  5.9 6.0 %front.1 = (s32[128,64]{1,0:T(8,128)S(1)}, f32[128,1,128]{2,1,0:T(1,128)S(1)}, f32[8,512]{1,0:T(8,128)S(1)}, bf16[32,2048]{1,0:T(8,128)(2,1)S(1)}, bf16[32,2048]{1,0:T(8,128)(2,1)S(1)}) custom-call(s32[1,1]{1,0:T(1,128)S(6)} %copy.9.id_ref, f32[1,1]{1,0:T(1,128)S(6)} %copy.10.inv_ref, s32[1,1]{1,0:T(1,128)S(6)} %copy.11.gap_ref, ...), custom_call_target="tpu_custom_call" | custom-call | tf_op jit(solution)/shard_map/front/pallas_call | solution.py:347
  12.0 0.0 copy-start.1
  12.0 1.2 %copy-done.1 = bf16[1,256,2048]{2,1,0:T(8,128)(2,1)S(1)} copy-done((bf16[1,256,2048]{2,1,0:T(8,128)(2,1)S(1)}, bf16[1,256,2048]{2,1,0:T(8,128)(2,1)}, u32[]{:S(2)}) %copy-start.1) | copy-done | bytes 1048600
  13.2 46.7 %fused.1 = (f32[512,1024]{1,0:T(8,128)S(1)}, f32[16,512]{1,0:T(8,128)S(1)}) custom-call(f32[1,1]{1,0:T(1,128)S(6)} %copy.10.inv_ref, s32[1,1]{1,0:T(1,128)S(6)} %copy.11.gap_ref, s32[128,64]{1,0:T(8,128)S(1)} %get-tuple-element.11.src_ref, f32[8,512]{1,0:T(8,128)S(1)} %get-tuple-element.12.taps_ref, bf16[32,2048]{1,0:T(8,128)(2,1)S(1)} %get-tuple-element.13.up_ref, ...), custom_call_target="tpu_custom_call" | custom-call | tf_op jit(solution)/shard_map/fused/pallas_call | solution.py:370
  59.9 2.2 %mean.1 = (f32[4096,128]{1,0:T(8,128)}, f32[1,4096]{1,0:T(1,128)}) custom-call(f32[512,1024]{1,0:T(8,128)S(1)} %get-tuple-element.16.total_ref, f32[16,512]{1,0:T(8,128)S(1)} %get-tuple-element.17.sums_ref), custom_call_target="tpu_custom_call" | custom-call | tf_op jit(solution)/shard_map/mean/pallas_call | solution.py:393
Async XLA Ops:
  2.6 1.2 %copy-start = (bf16[1,256,2048]{2,1,0:T(8,128)(2,1)S(1)}, bf16[1,256,2048]{2,1,0:T(8,128)(2,1)}, u32[]{:S(2)}) copy-start(bf16[1,256,2048]{2,1,0:T(8,128)(2,1)} %param.7) | copy-start | bytes 3145732
  3.8 0.7 %copy-start.2 = (s32[1,256,16,1]{1,3,2,0:T(1,128)S(1)}, s32[1,256,16,1]{1,3,2,0:T(1,128)}, u32[]{:S(2)}) copy-start(s32[1,256,16,1]{1,3,2,0:T(1,128)} %param.12) | copy-start | bytes 49156
  4.5 0.7 %copy-start.3 = (s32[1,256,16]{1,2,0:T(8,128)S(1)}, s32[1,256,16]{1,2,0:T(8,128)}, u32[]{:S(2)}) copy-start(s32[1,256,16]{1,2,0:T(8,128)} %param.13) | copy-start | bytes 49156
  5.2 0.7 %copy-start.4 = (bf16[8,2,41]{2,1,0:T(2,128)(2,1)S(1)}, bf16[8,2,41]{2,1,0:T(2,128)(2,1)}, u32[]{:S(2)}) copy-start(bf16[8,2,41]{2,1,0:T(2,128)(2,1)} %bank_hbm.1) | copy-start | bytes 3940
  12.0 1.2 %copy-start.1 = (bf16[1,256,2048]{2,1,0:T(8,128)(2,1)S(1)}, bf16[1,256,2048]{2,1,0:T(8,128)(2,1)}, u32[]{:S(2)}) copy-start(bf16[1,256,2048]{2,1,0:T(8,128)(2,1)} %param.7) | copy-start | bytes 3145732

commit v4 on v3

v4 whole, which is shorter than its diff:
```python
import jax
import jax.numpy as jnp
from jax import lax
from jax.experimental import pallas as pl
from jax.experimental.pallas import tpu as pltpu
from jax.sharding import PartitionSpec as P

GAP = 32
SEG = 128
CAP = 64
HALO = 32
FP = 32
DEVICES = 128
MESH = pl.DeviceIdType.MESH
NT = (((1,), (1,)), ((), ()))


def corner(group):
    y = lax.axis_index("expo")
    f = lax.axis_index("fp")
    b, c = lax.rem(group, 4), group // 4
    return y + c, f // 8 + b, lax.rem(f // 2, 4) + b + c, lax.rem(f, 2)


def target(at, i):
    y, x, z, core = at
    a = i // 2
    ty = lax.rem(y + a, 4)
    tf = lax.rem(x + a, 4) * 8 + lax.rem(z + a, 4) * 2 + lax.rem(core + i, 2)
    return ty, tf


def route(inv_ref, gap_ref, tile_ref, off_ref, src_ref, meta_ref):
    segs, _, rows = tile_ref.shape
    inv = inv_ref[0, 0]
    gap = gap_ref[0, 0]
    before = lax.broadcasted_iota(jnp.int32, (rows, rows), 0)
    after = lax.broadcasted_iota(jnp.int32, (rows, rows), 1)
    upper = (before < after).astype(jnp.float32).astype(jnp.bfloat16)
    tile_iota = lax.broadcasted_iota(jnp.int32, (DEVICES, rows), 0)
    slot_iota = lax.broadcasted_iota(jnp.int32, (CAP, rows), 0)
    row = lax.broadcasted_iota(jnp.int32, (1, rows), 1)
    open_row = jnp.where((row >= gap) & (row < gap + GAP), 0.0, 1.0)
    row_f = row.astype(jnp.float32)
    base = jnp.zeros((DEVICES, 1), jnp.float32)
    found = jnp.zeros((DEVICES, 5 * CAP), jnp.float32)
    for s in range(segs):
        hot = (tile_iota == tile_ref[s]).astype(jnp.float32)
        hot_b = hot.astype(jnp.bfloat16)
        inside = jnp.dot(hot_b, upper, preferred_element_type=jnp.float32)
        rank = jnp.sum(hot * (inside + base), axis=0, keepdims=True)
        base = base + jnp.sum(hot, axis=1, keepdims=True)
        at_slot = (slot_iota == rank.astype(jnp.int32)).astype(jnp.float32)
        offset = off_ref[s : s + 1, :] + 1
        packed = jnp.concatenate(
            [
                at_slot * float(s),
                at_slot * row_f,
                at_slot * (offset >> 6).astype(jnp.float32),
                at_slot * (offset & 63).astype(jnp.float32),
                at_slot * open_row,
            ],
            axis=0,
        ).astype(jnp.bfloat16)
        found = found + lax.dot_general(hot_b, packed, NT, preferred_element_type=jnp.float32)
    source = found[:, :CAP] * float(rows) + found[:, CAP : 2 * CAP]
    source = jnp.concatenate([source, jnp.zeros_like(source)], axis=1).astype(jnp.int32)
    src_ref[...] = jnp.clip(source, 0, segs * rows - 1)
    offset = found[:, 2 * CAP : 3 * CAP] * 64.0 + found[:, 3 * CAP : 4 * CAP] - 1.0
    meta_ref[:, 0, :] = jnp.concatenate([offset, found[:, 4 * CAP :] * inv], axis=1)


def band(taps, rows, width, shift):
    wide = jnp.broadcast_to(taps[:, :width], (rows, width))
    return pltpu.roll(wide, shift - 4, 1, stride=1, stride_axis=0).astype(jnp.bfloat16)


PARTS = 8
SPAN = 512
GROUP = 8
AHEAD = 5


def fused_kernel(
    id_ref, inv_ref, gap_ref, bank_hbm, tile_hbm, off_hbm, raw_ref, image_ref, weight_ref,
    total, weights,
    bank_ref, tile_ref, off_ref, taps_ref, slot_ref, src_ref, meta_ref, up_ref, down_ref,
    framed, vertical, pieces, stage, sent, got, gmeta,
    vsend, vrecv, msend, mrecv, edge_send, edge_recv, local, store,
):
    barrier = pltpu.get_barrier_semaphore()
    groups = DEVICES // GROUP

    y = lax.axis_index("expo")
    f = lax.axis_index("fp")
    rows, cols = raw_ref.shape
    half = SEG
    loads = [
        pltpu.make_async_copy(source, ref, local.at[n])
        for n, (source, ref) in enumerate(
            [
                (tile_hbm, tile_ref),
                (off_hbm, off_ref),
                (bank_hbm, bank_ref),
                (raw_ref, framed.at[pl.ds(64, rows)]),
            ]
        )
    ]
    for load in loads:
        load.start()
    ys = [lax.rem(y + k, 4) for k in range(4)]
    xs = [lax.rem(f // 8 + k, 4) * 8 for k in range(4)]
    zs = [lax.rem(f // 2 + k, 4) * 2 for k in range(4)]
    cores = [lax.rem(f + k, 2) for k in range(2)]
    others = []
    for step in range(1, DEVICES):
        a, b, c = step // 2 % 4, step // 8 % 4, step // 32
        to = (ys[(a + c) % 4], xs[(a + b) % 4] + zs[(a + b + c) % 4] + cores[step % 2])
        others.append(to)
        pl.semaphore_signal(barrier, inc=1, device_id=to, device_id_type=MESH)
    framed[0:64, :] = jnp.zeros((64, cols), jnp.bfloat16)
    framed[64 + rows : 128 + rows, :] = jnp.zeros((64, cols), jnp.bfloat16)
    for load in loads[:3]:
        load.wait()
    route(inv_ref, gap_ref, tile_ref, off_ref, slot_ref, meta_ref)
    to_scalars = pltpu.make_async_copy(slot_ref, src_ref, local.at[4])
    to_scalars.start()
    taps_ref[...] = jnp.zeros_like(taps_ref)
    taps_ref[0:2, 4 : 4 + bank_ref.shape[2]] = bank_ref[id_ref[0, 0]].astype(jnp.float32)
    vtap = taps_ref[0:1, :]
    htap = taps_ref[1:2, :]
    vertical[:, :SEG] = jnp.zeros((rows, SEG), jnp.bfloat16)
    vertical[:, SEG + cols :] = jnp.zeros((rows, SEG), jnp.bfloat16)
    vband = band(vtap, half, 256, 44)
    hband = band(htap, 256, 512, 108)
    loads[3].wait()
    for n in range(cols // 512):
        for m in range(rows // half):
            made = jnp.dot(
                vband,
                framed[m * half : m * half + 256, n * 512 : (n + 1) * 512],
                preferred_element_type=jnp.float32,
            )
            vertical[m * half : (m + 1) * half, SEG + n * 512 : SEG + (n + 1) * 512] = made.astype(
                jnp.bfloat16
            )
    row = lax.broadcasted_iota(jnp.int32, (rows, 256), 0)
    gap = gap_ref[0, 0]
    weight = jnp.where((row >= gap) & (row < gap + GAP), 0.0, inv_ref[0, 0])
    for n in range(cols // 256):
        made = lax.dot_general(
            vertical[:, n * 256 : n * 256 + 512], hband, NT, preferred_element_type=jnp.float32
        )
        made = made.astype(jnp.bfloat16).astype(jnp.float32) * weight
        pieces[2 * n * rows : (2 * n + 1) * rows, :] = made[:, :SEG]
        pieces[(2 * n + 1) * rows : (2 * n + 2) * rows, :] = made[:, SEG:]

    me = y * FP + f
    own_meta = pltpu.make_async_copy(meta_ref.at[me], gmeta.at[0], local.at[5])
    own = pltpu.make_async_copy(sent.at[0], got.at[0], local.at[6])
    own_meta.start()
    to_next = pltpu.make_async_remote_copy(
        src_ref=framed.at[pl.ds(32 + rows, HALO)], dst_ref=up_ref,
        send_sem=edge_send.at[0], recv_sem=edge_recv.at[0],
        device_id=(y, f + 1), device_id_type=MESH,
    )
    to_last = pltpu.make_async_remote_copy(
        src_ref=framed.at[pl.ds(64, HALO)], dst_ref=down_ref,
        send_sem=edge_send.at[1], recv_sem=edge_recv.at[1],
        device_id=(y, f - 1), device_id_type=MESH,
    )
    pl.semaphore_wait(barrier, DEVICES - 1)

    @pl.when(f < FP - 1)
    def _():
        to_next.start()

    @pl.when(f > 0)
    def _():
        to_last.start()

    for step in range(1, DEVICES):
        ty, tf = others[step - 1]
        pltpu.make_async_remote_copy(
            src_ref=meta_ref.at[ty * FP + tf], dst_ref=gmeta.at[step],
            send_sem=msend, recv_sem=mrecv,
            device_id=(ty, tf), device_id_type=MESH,
        ).start()
    top_band = band(vtap, HALO, SEG, 12)
    bottom_band = band(vtap, HALO, SEG, 44)

    @pl.when(f < FP - 1)
    def _():
        to_next.wait_send()
        to_last.wait_recv()
        framed[64 + rows : 96 + rows, :] = down_ref[...]

    @pl.when(f > 0)
    def _():
        to_last.wait_send()
        to_next.wait_recv()
        framed[32:64, :] = up_ref[...]

    made = jnp.dot(top_band, framed[32 : 32 + SEG, :], preferred_element_type=jnp.float32)
    vertical[:HALO, SEG : SEG + cols] = made.astype(jnp.bfloat16)
    made = jnp.dot(
        bottom_band, framed[rows - HALO : rows - HALO + SEG, :], preferred_element_type=jnp.float32
    )
    vertical[rows - HALO :, SEG : SEG + cols] = made.astype(jnp.bfloat16)
    edge_weight = jnp.concatenate([weight[:HALO], weight[rows - HALO :]], axis=0)
    for n in range(cols // 256):
        span = slice(n * 256, n * 256 + 512)
        both = jnp.concatenate([vertical[:HALO, span], vertical[rows - HALO :, span]], axis=0)
        made = lax.dot_general(both, hband, NT, preferred_element_type=jnp.float32)
        made = made.astype(jnp.bfloat16).astype(jnp.float32) * edge_weight
        for s in range(2):
            first = (2 * n + s) * rows
            lanes = slice(s * SEG, (s + 1) * SEG)
            pieces[first : first + HALO, :] = made[:HALO, lanes]
            pieces[first + rows - HALO : first + rows, :] = made[HALO:, lanes]
    to_scalars.wait()

    def value_copy(j, i, at):
        step = j * GROUP + i
        ty, tf = target(at, i)
        return pltpu.make_async_remote_copy(
            src_ref=sent.at[step], dst_ref=got.at[step],
            send_sem=vsend, recv_sem=vrecv.at[j],
            device_id=(ty, tf), device_id_type=MESH,
        )

    last_piece = pieces.shape[0] - 1

    def pack(j, carry):
        at = corner(j)
        for i in range(GROUP):
            ty, tf = target(at, i)
            to = ty * FP + tf
            for k in range(CAP):
                piece = jnp.clip(src_ref[to, k], 0, last_piece)
                stage[i, k : k + 1, :] = pieces[pl.ds(piece, 1), :]
            sent[j * GROUP + i] = stage[i].astype(jnp.bfloat16)
            if i:
                value_copy(j, i, at).start()
            else:

                @pl.when(j > 0)
                def _():
                    value_copy(j, 0, at).start()

                @pl.when(j == 0)
                def _():
                    own.start()

        return carry

    lax.fori_loop(0, AHEAD, pack, 0)
    span_iota = lax.broadcasted_iota(jnp.int32, (SPAN, GROUP * CAP), 0).astype(jnp.int16)
    part_iota = lax.broadcasted_iota(jnp.int32, (2 * PARTS, GROUP * CAP), 0)
    total[...] = jnp.zeros_like(total)
    weights[...] = jnp.zeros_like(weights)

    own_meta.wait()
    others_meta = gmeta.at[pl.ds(1, DEVICES - 1)]
    pltpu.make_async_copy(others_meta, others_meta, mrecv).wait()

    def arrived(j, first, count):
        slots = got.at[pl.ds(j * GROUP + first, count)]
        pltpu.make_async_copy(slots, slots, vrecv.at[j]).wait()

    def chunk(j, carry):
        @pl.when(j > 0)
        def _():
            arrived(j, 0, GROUP)

        @pl.when(j == 0)
        def _():
            own.wait()
            arrived(0, 1, GROUP - 1)

        meta = gmeta[pl.ds(j * GROUP, GROUP), 0, :]
        slots = jnp.concatenate([meta[i : i + 1, :CAP] for i in range(GROUP)], axis=1)
        weight = jnp.concatenate([meta[i : i + 1, CAP:] for i in range(GROUP)], axis=1)
        slots = slots.astype(jnp.int32)
        inside = jnp.broadcast_to(slots & (SPAN - 1), (16, GROUP * CAP)).astype(jnp.int16)
        inside = jnp.broadcast_to(inside[:1], (SPAN, GROUP * CAP))
        hot = jnp.where(span_iota == inside, jnp.bfloat16(1), jnp.bfloat16(0))
        high = weight.astype(jnp.bfloat16).astype(jnp.float32)
        part = slots >> 9
        spread = jnp.where(part_iota == part, high, 0.0)
        spread = jnp.where((part_iota == part + PARTS) & (part >= 0), weight - high, spread)
        weights[...] += lax.dot_general(
            spread.astype(jnp.bfloat16), hot, NT, preferred_element_type=jnp.float32
        )
        turned = jnp.floor(meta * (1.0 / SPAN)).T
        column = jnp.concatenate([turned[:CAP, i : i + 1] for i in range(GROUP)], axis=0)
        part = jnp.broadcast_to(column, (GROUP * CAP, SEG)).astype(jnp.bfloat16)
        values = got[pl.ds(j * GROUP, GROUP)].reshape(GROUP * CAP, SEG)
        none = jnp.zeros_like(values)
        masked = [jnp.where(part == jnp.bfloat16(a), values, none) for a in range(PARTS)]
        right = jnp.concatenate(masked, axis=1)
        total[...] += jnp.dot(hot, right, preferred_element_type=jnp.float32)
        return carry

    def both(j, carry):
        pack(j + AHEAD, carry)
        return chunk(j, carry)

    lax.fori_loop(0, groups - AHEAD, both, 0)
    lax.fori_loop(groups - AHEAD, groups, chunk, 0)

    sums = weights[:PARTS, :] + weights[PARTS:, :]
    scale = (1.0 / jnp.maximum(sums, 1.0)).T
    stores = []
    for a in range(PARTS):
        lanes = slice(a * SEG, (a + 1) * SEG)
        total[:, lanes] = total[:, lanes] * scale[:, a : a + 1]
        stores.append(
            pltpu.make_async_copy(
                total.at[:, pl.ds(a * SEG, SEG)], image_ref.at[pl.ds(a * SPAN, SPAN)], store.at[a]
            )
        )
        stores[-1].start()
        weight_ref[:, a * SPAN : (a + 1) * SPAN] = sums[a : a + 1, :]
    for copy in stores:
        copy.wait()
    for buffer, sem in ((meta_ref, msend), (sent, vsend)):
        slots = buffer.at[pl.ds(1, DEVICES - 1)]
        pltpu.make_async_copy(slots, slots, sem).wait()


def body(raw_pixels, kernel_bank, kernel_ids, inv_var, gap_start, warp_tile, warp_offset):
    raw = raw_pixels[0]
    rows, cols = raw.shape
    tiles = jnp.transpose(warp_tile[0], (1, 2, 0))
    offsets = warp_offset[0].T
    smem = pl.BlockSpec(memory_space=pltpu.SMEM)
    vmem = pl.BlockSpec(memory_space=pltpu.VMEM)
    fixed = pl.BlockSpec(memory_space=pltpu.HBM)
    dma = pltpu.SemaphoreType.DMA
    image, weight = pl.pallas_call(
        fused_kernel,
        out_shape=(
            jax.ShapeDtypeStruct((PARTS * SPAN, SEG), jnp.float32),
            jax.ShapeDtypeStruct((1, PARTS * SPAN), jnp.float32),
        ),
        in_specs=[smem, smem, smem, fixed, fixed, fixed, fixed],
        out_specs=(fixed, vmem),
        scratch_shapes=[
            pltpu.VMEM((SPAN, PARTS * SEG), jnp.float32),
            pltpu.VMEM((2 * PARTS, SPAN), jnp.float32),
            pltpu.VMEM(kernel_bank.shape, kernel_bank.dtype),
            pltpu.VMEM(tiles.shape, tiles.dtype),
            pltpu.VMEM(offsets.shape, offsets.dtype),
            pltpu.VMEM((8, 512), jnp.float32),
            pltpu.VMEM((DEVICES, 2 * CAP), jnp.int32),
            pltpu.SMEM((DEVICES, 2 * CAP), jnp.int32),
            pltpu.VMEM((DEVICES, 1, 2 * CAP), jnp.float32),
            pltpu.VMEM((HALO, cols), jnp.bfloat16),
            pltpu.VMEM((HALO, cols), jnp.bfloat16),
            pltpu.VMEM((rows + 128, cols), jnp.bfloat16),
            pltpu.VMEM((rows, cols + 2 * SEG), jnp.bfloat16),
            pltpu.VMEM((rows * cols // SEG, SEG), jnp.float32),
            pltpu.VMEM((GROUP, CAP, SEG), jnp.float32),
            pltpu.VMEM((DEVICES, CAP, SEG), jnp.bfloat16),
            pltpu.VMEM((DEVICES, CAP, SEG), jnp.bfloat16),
            pltpu.VMEM((DEVICES, 1, 2 * CAP), jnp.float32),
            dma, dma((DEVICES // GROUP,)), dma, dma, dma((2,)), dma((2,)), dma((7,)), dma((PARTS,)),
        ],
        compiler_params=pltpu.CompilerParams(
            collective_id=0, has_side_effects=True, vmem_limit_bytes=60 << 20
        ),
        name="fused",
    )(kernel_ids, inv_var, gap_start, kernel_bank, tiles, offsets, raw)
    return image[None], weight


def solution(mesh):
    in_specs = (
        P("expo", "fp", None),
        P(),
        P("expo", "fp"),
        P("expo", "fp"),
        P("expo", "fp"),
        P("expo", "fp", None, None),
        P("expo", "fp", None),
    )
    out_specs = (P(("expo", "fp"), None, None), P(("expo", "fp"), None))
    return jax.shard_map(body, mesh=mesh, in_specs=in_specs, out_specs=out_specs, check_vma=False)
```

time: 62.5 us -> 61.1 us (0.978)
  the two profiles are of different devices: /device:TPU:35 before, /device:TPU:1 now
where the time goes in v4:
time: 61.1 us; the launch traced here: 60.9 us
  Pallas kernels  54.6 us (89%)
  local copies, waits for them, and re-layouts  3.66 us (6%)
  between operations  2.58 us (4%)
    pallas_call x1, Pallas kernels, body(): pl.pallas_call(fused_kernel, out_shape=(jax.ShapeDtypeStruct((PARTS * SPA...  54.6 us
    unnamed x4, local copies, waits for them, and re-layouts  3.66 us

profile of v4, /device:TPU:1, one launch (start us, length us, event | category | flops | bytes accessed | tf_op | source)
XLA Modules:
  0.0 60.9 jit_solution(12061694704130034963)
XLA Ops:
  2.6 54.6 %fused.1 = (f32[4096,128]{1,0:T(8,128)}, f32[1,4096]{1,0:T(1,128)}) custom-call(s32[1,1]{1,0:T(1,128)S(6)} %copy.11.id_ref, f32[1,1]{1,0:T(1,128)S(6)} %copy.12.inv_ref, s32[1,1]{1,0:T(1,128)S(6)} %copy.13.gap_ref, bf16[8,2,41]{2,1,0:T(2,128)(2,1)} %bank_hbm.1, s32[16,1,256]{2,1,0:T(1,128)} %bitcast.10, s32[16,256]{1,0:T(8,128)} %bitcast.11, ...), custom_call_target="tpu_custom_call" | custom-call | tf_op jit(solution)/shard_map/fused/pallas_call | solution.py:341
  57.2 0.0 copy-start
  57.2 3.0 %copy.14 = f32[1,4096,128]{2,1,0:T(8,128)} copy(f32[1,4096,128]{2,1,0:T(8,128)} %bitcast.8) | data formatting | bytes 4194304
  60.3 0.0 copy-done
  60.3 0.6 copy.15
Async XLA Ops:
  57.2 3.1 %copy-start = (f32[1,4096]{1,0:T(1,128)S(1)}, f32[1,4096]{1,0:T(1,128)}, u32[]{:S(2)}) copy-start(f32[1,4096]{1,0:T(1,128)} %get-tuple-element.9) | copy-start | bytes 49156

commit v5 on v4

--- a/solution.py
+++ b/solution.py
@@ -229,16 +229,13 @@
             device_id=(ty, tf), device_id_type=MESH,
         )
 
-    last_piece = pieces.shape[0] - 1
-
     def pack(j, carry):
         at = corner(j)
         for i in range(GROUP):
             ty, tf = target(at, i)
             to = ty * FP + tf
             for k in range(CAP):
-                piece = jnp.clip(src_ref[to, k], 0, last_piece)
-                stage[i, k : k + 1, :] = pieces[pl.ds(piece, 1), :]
+                stage[i, k : k + 1, :] = pieces[pl.ds(src_ref[to, k], 1), :]
             sent[j * GROUP + i] = stage[i].astype(jnp.bfloat16)
             if i:
                 value_copy(j, i, at).start()

time: 61.1 us -> 56.2 us (0.920)
  Pallas kernels: 54.6 us -> 49.6 us
    pallas_call x1, Pallas kernels: 54.6 us -> 49.6 us  [body(): pl.pallas_call(fused_kernel, out_shape=(jax.ShapeDtypeStruct((PARTS * SPA...]
where the time goes in v5:
time: 56.2 us; the launch traced here: 55.9 us
  Pallas kernels  49.6 us (88%)
  local copies, waits for them, and re-layouts  3.66 us (7%)
  between operations  2.58 us (5%)
    pallas_call x1, Pallas kernels, body(): pl.pallas_call(fused_kernel, out_shape=(jax.ShapeDtypeStruct((PARTS * SPA...  49.6 us
    unnamed x4, local copies, waits for them, and re-layouts  3.66 us

profile of v5, /device:TPU:1, one launch (start us, length us, event | category | flops | bytes accessed | tf_op | source)
XLA Modules:
  0.0 55.9 jit_solution(8497589690604483022)
XLA Ops:
  2.6 49.6 %fused.1 = (f32[4096,128]{1,0:T(8,128)}, f32[1,4096]{1,0:T(1,128)}) custom-call(s32[1,1]{1,0:T(1,128)S(6)} %copy.11.id_ref, f32[1,1]{1,0:T(1,128)S(6)} %copy.12.inv_ref, s32[1,1]{1,0:T(1,128)S(6)} %copy.13.gap_ref, bf16[8,2,41]{2,1,0:T(2,128)(2,1)} %bank_hbm.1, s32[16,1,256]{2,1,0:T(1,128)} %bitcast.10, s32[16,256]{1,0:T(8,128)} %bitcast.11, ...), custom_call_target="tpu_custom_call" | custom-call | tf_op jit(solution)/shard_map/fused/pallas_call | solution.py:338
  52.2 0.0 copy-start
  52.2 3.0 %copy.14 = f32[1,4096,128]{2,1,0:T(8,128)} copy(f32[1,4096,128]{2,1,0:T(8,128)} %bitcast.8) | data formatting | bytes 4194304
  55.3 0.0 copy-done
  55.3 0.6 %copy.15 = f32[1,4096]{1,0:T(1,128)} copy(f32[1,4096]{1,0:T(1,128)S(1)} %copy-done) | data formatting | bytes 32768
Async XLA Ops:
  52.2 3.1 %copy-start = (f32[1,4096]{1,0:T(1,128)S(1)}, f32[1,4096]{1,0:T(1,128)}, u32[]{:S(2)}) copy-start(f32[1,4096]{1,0:T(1,128)} %get-tuple-element.9) | copy-start | bytes 49156
